TPU v7x, 512 devices: a whole 4x8x8 slice. The times are simulated.
512 devices in a mesh: section: 16 (over y, core), expert: 32 (over z, x).
Axes of the slice: x: 4, y: 8, z: 8, core: 2. Of those that a mesh axis runs over, the one named last changes fastest.
Arguments:
- pending: bfloat16 [2, 16, 2048, 3584], P(None, 'section', 'expert'), may hold values from -6 to 6
- routes: int32 [2, 16, 2048, 1], P(None, 'section', 'expert'), may hold values from 0 to 3; in each aligned block of 64 rows (0 to 63, 64 to 127, ..., all dimensions but the last counted through in order) at most 16 rows name the same one
- probs: bfloat16 [2, 16, 2048], P(None, 'section', 'expert'), may hold values from 0.049804688 to 0.94921875
- saved_gate: bfloat16 [2, 16, 32, 32, 16, 128], P(None, 'section', 'expert'), may hold values from -6 to 6
- saved_up: bfloat16 [2, 16, 32, 32, 16, 128], P(None, 'section', 'expert'), may hold values from -6 to 6
- w_gate: bfloat16 [16, 3584, 4096], P('section', None, 'expert'), may hold values from -0.09375 to 0.09375
- w_up: bfloat16 [16, 3584, 4096], P('section', None, 'expert'), may hold values from -0.09375 to 0.09375
- w_down: bfloat16 [16, 4096, 3584], P('section', 'expert'), may hold values from -0.09375 to 0.09375
- w_router: float32 [16, 3584, 4], P('section'), may hold values from -0.2 to 0.2
Outputs:
- passed: bfloat16 [2, 16, 2048, 3584], P(None, 'section', 'expert')
Inputs may be any that keep to these rules, and one draw needn't show every extreme that they name: `routes`: among the 64 tokens of one device, at one section and direction, each expert is chosen by exactly 16 tokens.
All inputs are finite; a program needn't handle non-finite values.
Results may differ from a plain program's by a relative error of at most 0.0031.
Values may be sent and summed in bfloat16 or wider, within the bound.
No kernel may reach another device: no remote copies, remote signals or barrier semaphores. Data moves between devices by JAX's collectives and lax.ppermute only.
A program may use at most 64 MiB of HBM per device.

v0:
```python
import jax
import jax.numpy as jnp
from jax import lax
from jax.sharding import PartitionSpec as P


def shifted(value, axis, steps):
    count = lax.axis_size(axis)
    pairs = [(source, (source + steps) % count) for source in range(count)]
    return lax.ppermute(value, axis, pairs)


def slot_tables(expert_ids, experts, capacity):
    onehot = (expert_ids[:, None] == jnp.arange(experts, dtype=jnp.int32)[None, :]).astype(
        jnp.int32
    )
    slot_index = jnp.sum((jnp.cumsum(onehot, axis=0) - 1) * onehot, axis=1)
    dest_code = expert_ids * capacity + slot_index
    selection = dest_code[:, None] == jnp.arange(experts * capacity, dtype=jnp.int32)[None, :]
    return (selection, onehot)


def outgoing(grad_in, prob, selection, experts, group, capacity):
    width = grad_in.shape[1]
    picked = lax.dot_general(
        selection.astype(jnp.bfloat16),
        grad_in,
        (((0,), (0,)), ((), ())),
        preferred_element_type=jnp.float32,
    ).astype(jnp.bfloat16)
    picked = jnp.broadcast_to(
        picked.reshape(experts, 1, capacity, width), (experts, group, capacity, width)
    )
    prob_slot = lax.dot_general(
        selection.astype(jnp.bfloat16),
        prob.reshape(-1, 1),
        (((0,), (0,)), ((), ())),
        preferred_element_type=jnp.float32,
    ).astype(jnp.bfloat16)
    prob_slot = jnp.broadcast_to(
        prob_slot.reshape(experts, 1, capacity), (experts, group, capacity)
    )
    return (
        picked.reshape(experts * group, capacity, width),
        prob_slot.reshape(experts * group, capacity),
    )


def expert_back(received, got_prob, gate_pre, up_pre, w_gate_dev, w_up_dev, w_down_dev):
    members, capacity, width = received.shape
    flat_rows = received.reshape(members * capacity, width)
    grad_z = lax.dot_general(
        flat_rows, w_down_dev, (((1,), (1,)), ((), ())), preferred_element_type=jnp.float32
    )
    gate_f = gate_pre.reshape(members * capacity, -1).astype(jnp.float32)
    up_f = up_pre.reshape(members * capacity, -1).astype(jnp.float32)
    sig = jax.nn.sigmoid(gate_f)
    hidden = gate_f * sig * up_f
    dots = jnp.sum(hidden * grad_z, axis=1).astype(jnp.bfloat16)
    grad_h = got_prob.reshape(-1).astype(jnp.float32)[:, None] * grad_z
    grad_gate = (grad_h * up_f * sig * (1.0 + gate_f * (1.0 - sig))).astype(jnp.bfloat16)
    grad_up = (grad_h * gate_f * sig).astype(jnp.bfloat16)
    parts = lax.dot_general(
        grad_gate, w_gate_dev, (((1,), (1,)), ((), ())), preferred_element_type=jnp.float32
    )
    parts = parts + lax.dot_general(
        grad_up, w_up_dev, (((1,), (1,)), ((), ())), preferred_element_type=jnp.float32
    )
    return (
        parts.astype(jnp.bfloat16).reshape(members, capacity, width),
        dots.reshape(members, capacity),
    )


def finish(parts, dots, selection, onehot, grad_in, prob, w_router_dev, experts, group, capacity):
    width = grad_in.shape[1]
    summed = jnp.sum(parts.reshape(experts, group, capacity, width).astype(jnp.float32), axis=1)
    dot_total = jnp.sum(dots.reshape(experts, group, capacity).astype(jnp.float32), axis=1)
    select_f = selection.astype(jnp.float32)
    back = jnp.dot(
        select_f, summed.reshape(experts * capacity, width), precision=lax.Precision.HIGHEST
    )
    dot_tok = jnp.dot(select_f, dot_total.reshape(-1), precision=lax.Precision.HIGHEST)
    prob_f = prob.astype(jnp.float32)
    scaled = dot_tok * prob_f * (1.0 - prob_f)
    router_term = jnp.dot(
        onehot.astype(jnp.float32) * scaled[:, None],
        jnp.transpose(w_router_dev),
        precision=lax.Precision.HIGHEST,
    )
    return (grad_in.astype(jnp.float32) + back + router_term).astype(jnp.bfloat16)


def per_device(pending, routes, probs, saved_gate, saved_up, w_gate, w_up, w_down, w_router):
    members = lax.axis_size("expert")
    experts = w_router.shape[2]
    group = members // experts
    tok_count = pending.shape[2]
    capacity = tok_count // experts
    from_above = shifted(pending[0, 0], "section", -1)
    from_below = shifted(pending[1, 0], "section", 1)
    incoming = (from_above, from_below)
    w_gate_dev = w_gate[0]
    w_up_dev = w_up[0]
    w_down_dev = w_down[0]
    w_router_dev = w_router[0]
    tables = [slot_tables(routes[direction, 0, :, 0], experts, capacity) for direction in range(2)]
    sends = [
        outgoing(
            incoming[direction], probs[direction, 0], tables[direction][0], experts, group, capacity
        )
        for direction in range(2)
    ]
    results = []
    for direction in range(2):
        received = lax.all_to_all(
            sends[direction][0], "expert", split_axis=0, concat_axis=0, tiled=True
        )
        got_prob = lax.all_to_all(
            sends[direction][1], "expert", split_axis=0, concat_axis=0, tiled=True
        )
        parts, dots = expert_back(
            received,
            got_prob,
            saved_gate[direction, 0, 0],
            saved_up[direction, 0, 0],
            w_gate_dev,
            w_up_dev,
            w_down_dev,
        )
        parts, dots = (
            lax.all_to_all(parts, "expert", split_axis=0, concat_axis=0, tiled=True),
            lax.all_to_all(dots, "expert", split_axis=0, concat_axis=0, tiled=True),
        )
        results.append(
            finish(
                parts,
                dots,
                tables[direction][0],
                tables[direction][1],
                incoming[direction],
                probs[direction, 0],
                w_router_dev,
                experts,
                group,
                capacity,
            )
        )
    return jnp.stack(results)[:, None]


def solution(mesh):
    in_specs = (
        P(None, "section", "expert", None),
        P(None, "section", "expert", None),
        P(None, "section", "expert"),
        P(None, "section", "expert", None, None, None),
        P(None, "section", "expert", None, None, None),
        P("section", None, "expert"),
        P("section", None, "expert"),
        P("section", "expert", None),
        P("section", None, None),
    )
    out_specs = P(None, "section", "expert", None)
    return jax.shard_map(
        per_device, mesh=mesh, in_specs=in_specs, out_specs=out_specs, check_vma=False
    )
```

profile of v0, /device:TPU:10, one launch (start us, length us, event | category | flops | bytes accessed | tf_op | source)
XLA Modules:
  0.0 430.7 jit_solution(4727751966108540951)
XLA Ops:
  0.0 1.3 slice_bitcast_fusion.1
  1.3 0.7 slice_bitcast_fusion.3
  2.0 0.1 fusion.41
  2.1 0.1 fusion.37
  2.2 0.1 reduce_window_sum.17
  2.3 0.1 reduce_window_sum.18
  2.4 0.2 select_reduce_fusion
  2.5 0.7 multiply_add_fusion.1
  3.2 0.8 fusion.2
  4.1 0.1 broadcast_in_dim.18
  4.2 0.6 copy.43
  4.8 13.5 %all-to-all-start = ((bf16[32,1,16]{2,1,0:T(2,128)(2,1)}), bf16[32,1,16]{2,1,0:T(2,128)(2,1)S(1)}, u32[]{:S(2)}, u32[]{:S(2)}) async-start(bf16[32,1,16]{2,1,0:T(2,128)(2,1)} %copy.43), calls=%async_computation | async-start | bytes 32768 | tf_op jit(solution)/shard_map/all_to_all | solution.py:119
  18.2 0.8 fusion.4
  19.1 0.1 broadcast_in_dim.22
  19.2 0.6 copy.51
  19.8 6.9 %all-to-all-done = bf16[32,1,16]{2,1,0:T(2,128)(2,1)S(1)} async-done(((bf16[32,1,16]{2,1,0:T(2,128)(2,1)}), bf16[32,1,16]{2,1,0:T(2,128)(2,1)S(1)}, u32[]{:S(2)}, u32[]{:S(2)}) %all-to-all-start) | async-done | bytes 1056 | tf_op jit(solution)/shard_map/all_to_all | solution.py:119
  26.8 4.8 %all-to-all-start.4 = ((bf16[32,1,16]{2,1,0:T(2,128)(2,1)}), bf16[32,1,16]{2,1,0:T(2,128)(2,1)S(1)}, u32[]{:S(2)}, u32[]{:S(2)}) async-start(bf16[32,1,16]{2,1,0:T(2,128)(2,1)} %copy.51), calls=%async_computation.4 | async-start | bytes 32768 | tf_op jit(solution)/shard_map/all_to_all | solution.py:119
  31.6 0.4 convolution_convert_fusion.1
  32.0 8.1 %all-to-all-done.4 = bf16[32,1,16]{2,1,0:T(2,128)(2,1)S(1)} async-done(((bf16[32,1,16]{2,1,0:T(2,128)(2,1)}), bf16[32,1,16]{2,1,0:T(2,128)(2,1)S(1)}, u32[]{:S(2)}, u32[]{:S(2)}) %all-to-all-start.4) | async-done | bytes 1056 | tf_op jit(solution)/shard_map/all_to_all | solution.py:119
  40.1 2.2 broadcast_in_dim.21
  42.4 5.9 %all-to-all-start.1 = ((bf16[32,16,3584]{2,1,0:T(8,128)(2,1)}), bf16[32,16,3584]{2,1,0:T(8,128)(2,1)}, u32[]{:S(2)}, u32[]{:S(2)}) async-start(bf16[32,16,3584]{2,1,0:T(8,128)(2,1)} %bitcast.141), calls=%async_computation.1 | async-start | bytes 7340032 | tf_op jit(solution)/shard_map/all_to_all | solution.py:116
  48.3 7.9 %collective-permute-done.1 = bf16[64,3584]{1,0:T(8,128)(2,1)S(1)} collective-permute-done((bf16[64,3584]{1,0:T(8,128)(2,1)S(1)}, bf16[64,3584]{1,0:T(8,128)(2,1)S(1)}, u32[]{:S(2)}, u32[]{:S(2)}) %collective-permute-start.1) | collective-permute-done | bytes 458784 | tf_op jit(solution)/shard_map/ppermute | solution.py:10
  56.2 0.4 convolution_convert_fusion
  56.6 73.2 %all-to-all-done.1 = bf16[32,16,3584]{2,1,0:T(8,128)(2,1)} async-done(((bf16[32,16,3584]{2,1,0:T(8,128)(2,1)}), bf16[32,16,3584]{2,1,0:T(8,128)(2,1)}, u32[]{:S(2)}, u32[]{:S(2)}) %all-to-all-start.1) | async-done | bytes 3670048 | tf_op jit(solution)/shard_map/all_to_all | solution.py:116
  129.8 2.3 broadcast_in_dim.48
  132.1 7.1 %all-to-all-start.5 = ((bf16[32,16,3584]{2,1,0:T(8,128)(2,1)}), bf16[32,16,3584]{2,1,0:T(8,128)(2,1)}, u32[]{:S(2)}, u32[]{:S(2)}) async-start(bf16[32,16,3584]{2,1,0:T(8,128)(2,1)} %bitcast.138), calls=%async_computation.5 | async-start | bytes 7340032 | tf_op jit(solution)/shard_map/all_to_all | solution.py:116
  139.3 0.1 copy.45
  139.5 0.1 copy.44
  139.7 0.1 copy.53
  139.9 0.8 copy.52
  140.7 0.1 convert_reduce_fusion.3
  140.8 0.1 reshape.162
  140.9 3.6 multiply_reduce_fusion.1
  144.5 0.7 convert_element_type.224
  145.2 4.1 fusion.10
  149.3 72.1 %all-to-all-done.5 = bf16[32,16,3584]{2,1,0:T(8,128)(2,1)} async-done(((bf16[32,16,3584]{2,1,0:T(8,128)(2,1)}), bf16[32,16,3584]{2,1,0:T(8,128)(2,1)}, u32[]{:S(2)}, u32[]{:S(2)}) %all-to-all-start.5) | async-done | bytes 3670048 | tf_op jit(solution)/shard_map/all_to_all | solution.py:116
  221.4 5.9 %all-to-all-start.3 = ((bf16[32,1,16]{2,1,0:T(2,128)(2,1)}), bf16[32,1,16]{2,1,0:T(2,128)(2,1)}, u32[]{:S(2)}, u32[]{:S(2)}) async-start(bf16[32,1,16]{2,1,0:T(2,128)(2,1)} %convert_element_type.224), calls=%async_computation.3 | async-start | bytes 32768 | tf_op jit(solution)/shard_map/all_to_all | solution.py:133
  227.3 3.6 multiply_reduce_fusion
  231.0 0.7 convert_element_type.225
  231.7 4.2 all-to-all-done.3
  235.9 5.6 %all-to-all-start.7 = ((bf16[32,1,16]{2,1,0:T(2,128)(2,1)}), bf16[32,1,16]{2,1,0:T(2,128)(2,1)}, u32[]{:S(2)}, u32[]{:S(2)}) async-start(bf16[32,1,16]{2,1,0:T(2,128)(2,1)} %convert_element_type.225), calls=%async_computation.7 | async-start | bytes 32768 | tf_op jit(solution)/shard_map/all_to_all | solution.py:133
  241.5 6.3 %add_convert_fusion.1 = bf16[512,3584]{1,0:T(8,128)(2,1)} fusion(f32[512,3584]{1,0:T(8,128)} %fusion.10, bf16[1,3584,128]{2,1,0:T(8,128)(2,1)S(1)} %copy-done.1, f32[512,128]{0,1:T(8,128)S(1)} %copy.45, f32[512,128]{0,1:T(8,128)} %copy-done.2, f32[512]{0:T(512)S(1)} %reshape.162), kind=kOutput, calls=%fused_computation.3 | convolution fusion | flops 473890816 | bytes 12453888 | tf_op jit(solution)/shard_map/dot_general | solution.py:66
  247.8 2.2 all-to-all-done.7
  250.0 7.8 %all-to-all-start.2 = ((bf16[32,16,3584]{2,1,0:T(8,128)(2,1)}), bf16[32,16,3584]{2,1,0:T(8,128)(2,1)}, u32[]{:S(2)}, u32[]{:S(2)}) async-start(bf16[32,16,3584]{2,1,0:T(8,128)(2,1)} %bitcast.140), calls=%async_computation.2 | async-start | bytes 7340032 | tf_op jit(solution)/shard_map/all_to_all | solution.py:132
  257.8 0.6 convert_reduce_fusion.2
  258.4 0.8 reshape.167
  259.2 1.2 fusion.8
  260.4 3.0 add_convert_fusion
  263.4 74.8 %all-to-all-done.2 = bf16[32,16,3584]{2,1,0:T(8,128)(2,1)} async-done(((bf16[32,16,3584]{2,1,0:T(8,128)(2,1)}), bf16[32,16,3584]{2,1,0:T(8,128)(2,1)}, u32[]{:S(2)}, u32[]{:S(2)}) %all-to-all-start.2) | async-done | bytes 3670048 | tf_op jit(solution)/shard_map/all_to_all | solution.py:132
  338.3 5.5 %all-to-all-start.6 = ((bf16[32,16,3584]{2,1,0:T(8,128)(2,1)}), bf16[32,16,3584]{2,1,0:T(8,128)(2,1)}, u32[]{:S(2)}, u32[]{:S(2)}) async-start(bf16[32,16,3584]{2,1,0:T(8,128)(2,1)} %bitcast.139), calls=%async_computation.6 | async-start | bytes 7340032 | tf_op jit(solution)/shard_map/all_to_all | solution.py:132
  343.8 0.7 convert_element_type.218
  344.5 0.1 reshape.174
  344.6 0.7 convert_element_type.223
  345.4 0.1 reshape.178
  345.5 0.2 fusion.3
  345.7 0.2 fusion.5
  345.9 2.7 convert_reduce_fusion.1
  348.6 0.6 fusion.40
  349.2 75.3 %all-to-all-done.6 = bf16[32,16,3584]{2,1,0:T(8,128)(2,1)} async-done(((bf16[32,16,3584]{2,1,0:T(8,128)(2,1)}), bf16[32,16,3584]{2,1,0:T(8,128)(2,1)}, u32[]{:S(2)}, u32[]{:S(2)}) %all-to-all-start.6) | async-done | bytes 3670048 | tf_op jit(solution)/shard_map/all_to_all | solution.py:132
  424.5 2.6 convert_reduce_fusion
  427.2 0.6 fusion.36
  427.8 0.9 fusion.16
  428.7 1.0 fusion.17
  429.7 1.0 maximum_bitcast_fusion
  (49 shorter events, 0.3 us)
Async XLA Ops:
  0.0 145.2 %copy-start = (bf16[1,3584,128]{2,1,0:T(8,128)(2,1)S(1)}, bf16[1,3584,128]{2,1,0:T(8,128)(2,1)}, u32[]{:S(2)}) copy-start(bf16[1,3584,128]{2,1,0:T(8,128)(2,1)} %param.14) | copy-start | bytes 2752516
  1.3 30.3 %collective-permute-start = (bf16[64,3584]{1,0:T(8,128)(2,1)S(1)}, bf16[64,3584]{1,0:T(8,128)(2,1)S(1)}, u32[]{:S(2)}, u32[]{:S(2)}) collective-permute-start(bf16[64,3584]{1,0:T(8,128)(2,1)S(1)} %get-tuple-element.5), channel_id=1, source_target_pairs={{0,480},{32,0},{64,32},{96,64},{128,96},{160,128},{192,160},{224,1... | collective-permute-start | bytes 1376264 | tf_op jit(solution)/shard_map/ppermute | solution.py:10
  2.0 40.4 %copy-start.9 = (s32[64]{0:T(128)}, s32[64]{0:T(128)S(1)}, u32[]{:S(2)}) copy-start(s32[64]{0:T(128)S(1)} %get-tuple-element.14) | copy-start | bytes 772
  2.0 40.4 %copy-start.11 = (s32[64]{0:T(128)}, s32[64]{0:T(128)S(1)}, u32[]{:S(2)}) copy-start(s32[64]{0:T(128)S(1)} %get-tuple-element.13) | copy-start | bytes 772
  3.2 39.2 %copy-start.15 = (s32[64]{0:T(128)}, s32[64]{0:T(128)S(1)}, u32[]{:S(2)}) copy-start(s32[64]{0:T(128)S(1)} %get-tuple-element.11) | copy-start | bytes 772
  3.2 53.0 %copy-start.13 = (s32[64]{0:T(128)}, s32[64]{0:T(128)S(1)}, u32[]{:S(2)}) copy-start(s32[64]{0:T(128)S(1)} %get-tuple-element.12) | copy-start | bytes 772
  4.8 22.0 %all-to-all-start = ((bf16[32,1,16]{2,1,0:T(2,128)(2,1)}), bf16[32,1,16]{2,1,0:T(2,128)(2,1)S(1)}, u32[]{:S(2)}, u32[]{:S(2)}) async-start(bf16[32,1,16]{2,1,0:T(2,128)(2,1)} %copy.43), calls=%async_computation | async-start | bytes 32768 | tf_op jit(solution)/shard_map/all_to_all | solution.py:119
  26.8 13.3 %all-to-all-start.4 = ((bf16[32,1,16]{2,1,0:T(2,128)(2,1)}), bf16[32,1,16]{2,1,0:T(2,128)(2,1)S(1)}, u32[]{:S(2)}, u32[]{:S(2)}) async-start(bf16[32,1,16]{2,1,0:T(2,128)(2,1)} %copy.51), calls=%async_computation.4 | async-start | bytes 32768 | tf_op jit(solution)/shard_map/all_to_all | solution.py:119
  40.1 2.3 copy-start.7
  42.4 87.4 %all-to-all-start.1 = ((bf16[32,16,3584]{2,1,0:T(8,128)(2,1)}), bf16[32,16,3584]{2,1,0:T(8,128)(2,1)}, u32[]{:S(2)}, u32[]{:S(2)}) async-start(bf16[32,16,3584]{2,1,0:T(8,128)(2,1)} %bitcast.141), calls=%async_computation.1 | async-start | bytes 7340032 | tf_op jit(solution)/shard_map/all_to_all | solution.py:116
  48.3 7.9 %collective-permute-start.1 = (bf16[64,3584]{1,0:T(8,128)(2,1)S(1)}, bf16[64,3584]{1,0:T(8,128)(2,1)S(1)}, u32[]{:S(2)}, u32[]{:S(2)}) collective-permute-start(bf16[64,3584]{1,0:T(8,128)(2,1)S(1)} %get-tuple-element.6), channel_id=1, source_target_pairs={{0,32},{32,64},{64,96},{96,128},{128,160},{160,192},{192,224},{224... | collective-permute-start | bytes 1376264 | tf_op jit(solution)/shard_map/ppermute | solution.py:10
  132.1 7.1 %copy-start.4 = (bf16[2,1,1,32,16,128]{5,4,3,2,1,0:T(8,128)(2,1)S(1)}, bf16[2,1,1,32,16,128]{5,4,3,2,1,0:T(8,128)(2,1)}, u32[]{:S(2)}) copy-start(bf16[2,1,1,32,16,128]{5,4,3,2,1,0:T(8,128)(2,1)} %param.12) | copy-start | bytes 786436
  132.1 7.3 %copy-start.5 = (bf16[2,1,1,32,16,128]{5,4,3,2,1,0:T(8,128)(2,1)S(1)}, bf16[2,1,1,32,16,128]{5,4,3,2,1,0:T(8,128)(2,1)}, u32[]{:S(2)}) copy-start(bf16[2,1,1,32,16,128]{5,4,3,2,1,0:T(8,128)(2,1)} %param.13) | copy-start | bytes 786436
  132.1 89.3 %all-to-all-start.5 = ((bf16[32,16,3584]{2,1,0:T(8,128)(2,1)}), bf16[32,16,3584]{2,1,0:T(8,128)(2,1)}, u32[]{:S(2)}, u32[]{:S(2)}) async-start(bf16[32,16,3584]{2,1,0:T(8,128)(2,1)} %bitcast.138), calls=%async_computation.5 | async-start | bytes 7340032 | tf_op jit(solution)/shard_map/all_to_all | solution.py:116
  144.4 0.7 copy-start.2
  149.3 92.2 %copy-start.1 = (bf16[1,3584,128]{2,1,0:T(8,128)(2,1)S(1)}, bf16[1,3584,128]{2,1,0:T(8,128)(2,1)}, u32[]{:S(2)}) copy-start(bf16[1,3584,128]{2,1,0:T(8,128)(2,1)} %param.15) | copy-start | bytes 2752516
  221.4 14.5 %all-to-all-start.3 = ((bf16[32,1,16]{2,1,0:T(2,128)(2,1)}), bf16[32,1,16]{2,1,0:T(2,128)(2,1)}, u32[]{:S(2)}, u32[]{:S(2)}) async-start(bf16[32,1,16]{2,1,0:T(2,128)(2,1)} %convert_element_type.224), calls=%async_computation.3 | async-start | bytes 32768 | tf_op jit(solution)/shard_map/all_to_all | solution.py:133
  235.9 14.0 %all-to-all-start.7 = ((bf16[32,1,16]{2,1,0:T(2,128)(2,1)}), bf16[32,1,16]{2,1,0:T(2,128)(2,1)}, u32[]{:S(2)}, u32[]{:S(2)}) async-start(bf16[32,1,16]{2,1,0:T(2,128)(2,1)} %convert_element_type.225), calls=%async_computation.7 | async-start | bytes 32768 | tf_op jit(solution)/shard_map/all_to_all | solution.py:133
  250.0 7.8 %copy-start.8 = (bf16[32,1,16]{2,1,0:T(2,128)(2,1)S(1)}, bf16[32,1,16]{2,1,0:T(2,128)(2,1)}, u32[]{:S(2)}) copy-start(bf16[32,1,16]{2,1,0:T(2,128)(2,1)} %copy-done.7) | copy-start | bytes 3076
  250.0 9.3 %copy-start.3 = (f32[512,128]{0,1:T(8,128)S(1)}, f32[512,128]{0,1:T(8,128)}, u32[]{:S(2)}) copy-start(f32[512,128]{0,1:T(8,128)} %copy.52) | copy-start | bytes 786436
  250.0 88.3 %all-to-all-start.2 = ((bf16[32,16,3584]{2,1,0:T(8,128)(2,1)}), bf16[32,16,3584]{2,1,0:T(8,128)(2,1)}, u32[]{:S(2)}, u32[]{:S(2)}) async-start(bf16[32,16,3584]{2,1,0:T(8,128)(2,1)} %bitcast.140), calls=%async_computation.2 | async-start | bytes 7340032 | tf_op jit(solution)/shard_map/all_to_all | solution.py:132
  338.3 7.2 %copy-start.16 = (s32[64]{0:T(128)S(1)}, s32[64]{0:T(128)}, u32[]{:S(2)}) copy-start(s32[64]{0:T(128)} %copy-done.15) | copy-start | bytes 772
  338.3 7.2 %copy-start.17 = (bf16[2,1,64]{2,0,1:T(2,128)(2,1)S(1)}, bf16[2,1,64]{2,0,1:T(2,128)(2,1)}, u32[]{:S(2)}) copy-start(bf16[2,1,64]{2,0,1:T(2,128)(2,1)} %param.11) | copy-start | bytes 772
  338.3 7.4 %copy-start.14 = (s32[64]{0:T(128)S(1)}, s32[64]{0:T(128)}, u32[]{:S(2)}) copy-start(s32[64]{0:T(128)} %copy-done.13) | copy-start | bytes 772
  338.3 86.2 %all-to-all-start.6 = ((bf16[32,16,3584]{2,1,0:T(8,128)(2,1)}), bf16[32,16,3584]{2,1,0:T(8,128)(2,1)}, u32[]{:S(2)}, u32[]{:S(2)}) async-start(bf16[32,16,3584]{2,1,0:T(8,128)(2,1)} %bitcast.139), calls=%async_computation.6 | async-start | bytes 7340032 | tf_op jit(solution)/shard_map/all_to_all | solution.py:132
  349.2 78.6 %copy-start.6 = (f32[1,3584,4]{1,2,0:T(4,128)S(1)}, f32[1,3584,4]{1,2,0:T(4,128)}, u32[]{:S(2)}) copy-start(f32[1,3584,4]{1,2,0:T(4,128)} %param.17) | copy-start | bytes 172036
  349.2 78.6 %copy-start.12 = (s32[64]{0:T(128)S(1)}, s32[64]{0:T(128)}, u32[]{:S(2)}) copy-start(s32[64]{0:T(128)} %copy-done.11) | copy-start | bytes 772
  349.2 79.5 %copy-start.10 = (s32[64]{0:T(128)S(1)}, s32[64]{0:T(128)}, u32[]{:S(2)}) copy-start(s32[64]{0:T(128)} %copy-done.9) | copy-start | bytes 772
where the time goes:
time: 432 us; the launch traced here: 431 us
  waiting for transfers between devices  325 us (75%)
  starting transfers between devices  56.1 us (13%)
  matrix products  27.8 us (6%)
  local copies, waits for them, and re-layouts  11.7 us (3%)
  other arithmetic  9.87 us (2%)
    all_to_all x2, waiting for transfers between devices, per_device(): lax.all_to_all(parts, 'expert', split_axis=0, concat_axis=0, tiled=True)  150 us
    all_to_all x2, waiting for transfers between devices, per_device(): lax.all_to_all(sends[direction][0], 'expert', split_axis=0, concat_axis=0...  145 us
    all_to_all x2, starting transfers between devices, per_device(): lax.all_to_all(sends[direction][1], 'expert', split_axis=0, concat_axis=0...  18.2 us
    all_to_all x2, waiting for transfers between devices, per_device(): lax.all_to_all(sends[direction][1], 'expert', split_axis=0, concat_axis=0...  15.1 us
    all_to_all x2, starting transfers between devices, per_device(): lax.all_to_all(parts, 'expert', split_axis=0, concat_axis=0, tiled=True)  13.3 us
    all_to_all x2, starting transfers between devices, per_device(): lax.all_to_all(sends[direction][0], 'expert', split_axis=0, concat_axis=0...  13 us
    all_to_all x2, starting transfers between devices, per_device(): lax.all_to_all(dots, 'expert', split_axis=0, concat_axis=0, tiled=True)  11.5 us
    dot_general x2, matrix products, expert_back(): lax.dot_general(grad_up, w_up_dev, (((1,), (1,)), ((), ())), preferred_el...  9.28 us
  transfers between devices with their start and end apart: 10, of which 9 were waited for; matrix products, arithmetic and copies ran while one was open for 9% of the time, Pallas kernels for 0%

commit v1 on v0

v1 whole, which is shorter than its diff:
```python
import functools

import jax
import jax.numpy as jnp
from jax import lax
from jax.experimental import pallas as pl
from jax.experimental.pallas import tpu as pltpu
from jax.sharding import PartitionSpec as P

BF = jnp.bfloat16
F32 = jnp.float32
LANE = 128
RING = 4
VMEM_LIMIT = 48 * 1024 * 1024


def shifted(value, axis, steps):
    count = lax.axis_size(axis)
    pairs = [(source, (source + steps) % count) for source in range(count)]
    return lax.ppermute(value, axis, pairs)


def turned(value, steps):
    count = lax.axis_size("expert")
    pairs = [(i, i - i % RING + (i + steps) % RING) for i in range(count)]
    return lax.ppermute(value, "expert", pairs)


def columns(count):
    return [[z * RING + x for z in range(count // RING)] for x in range(RING)]


def rows(count):
    return [[z * RING + x for x in range(RING)] for z in range(count // RING)]


def dot(a, b, contract):
    return lax.dot_general(a, b, ((contract[0], contract[1]), ((), ())), preferred_element_type=F32)


def selection(routes, copies, capacity, experts):
    count = routes.shape[0]
    width = experts * copies * capacity
    code = lax.broadcasted_iota(jnp.int32, (count, width), 1)
    chosen = routes == code // (copies * capacity)
    row = lax.broadcasted_iota(jnp.int32, (count, count), 0)
    col = lax.broadcasted_iota(jnp.int32, (count, count), 1)
    earlier = jnp.where(col < row, 1.0, 0.0).astype(BF)
    before = dot(earlier, jnp.where(chosen, 1.0, 0.0).astype(BF), ((1,), (0,)))
    return jnp.where(chosen & (before.astype(jnp.int32) == code % capacity), 1.0, 0.0)


def pick_kernel(experts, capacity, routes_ref, probs_ref, *rest):
    grads, outs = rest[:2], rest[2:]
    for way in range(2):
        tokens, width = grads[way].shape
        select = selection(routes_ref[way, 0], 1, capacity, experts)
        prob_row = jnp.broadcast_to(probs_ref[way].astype(F32), (tokens, tokens))
        row = lax.broadcasted_iota(jnp.int32, (tokens, tokens), 0)
        col = lax.broadcasted_iota(jnp.int32, (tokens, tokens), 1)
        prob_diag = jnp.where(row == col, prob_row, 0.0).astype(BF)
        select = select.astype(BF)
        prob = jnp.sum(dot(select, prob_diag, ((0,), (0,))), axis=1, keepdims=True)
        prob = jnp.broadcast_to(prob, (tokens, LANE)).astype(BF)
        step = width // RING
        for part in range(RING):
            span = slice(part * step, (part + 1) * step)
            picked = dot(select, grads[way][:, span], ((0,), (0,))).astype(BF)
            for place in range(2 * experts):
                first = place // 2 * capacity
                outs[way][place, :, span] = picked[first : first + capacity]
        for place in range(2 * experts):
            first = place // 2 * capacity
            outs[way][place, :, width:] = prob[first : first + capacity]


def pick(grads, routes, probs, experts, capacity):
    tokens, width = grads[0].shape
    return pl.pallas_call(
        functools.partial(pick_kernel, experts, capacity),
        out_shape=[jax.ShapeDtypeStruct((2 * experts, capacity, width + LANE), BF)] * 2,
        compiler_params=pltpu.CompilerParams(vmem_limit_bytes=VMEM_LIMIT),
        cost_estimate=pl.CostEstimate(flops=10**8, bytes_accessed=4 * 10**6, transcendentals=0),
    )(routes, probs, *grads)


def saved_kernel(gate_ref, up_ref, out_ref):
    planes, ring, capacity, units = gate_ref.shape[1:]
    for x in range(ring):
        for way in range(2):
            out_ref[x, way, 0] = gate_ref[way, :, x].reshape(planes * capacity, units)
            out_ref[x, way, 1] = up_ref[way, :, x].reshape(planes * capacity, units)


def saved_blocks(gate, up):
    _, senders, capacity, units = gate.shape
    planes = senders // RING
    gate = gate.reshape(2, planes, RING, capacity, units)
    up = up.reshape(2, planes, RING, capacity, units)
    return pl.pallas_call(
        saved_kernel,
        out_shape=jax.ShapeDtypeStruct((RING, 2, 2, planes * capacity, units), BF),
        compiler_params=pltpu.CompilerParams(vmem_limit_bytes=VMEM_LIMIT),
        cost_estimate=pl.CostEstimate(flops=0, bytes_accessed=2 * 10**6, transcendentals=0),
    )(gate, up)


def hidden_kernel(
    way, place_ref, tok_ref, saved_ref, own_ref, left_ref, right_ref, low_ref, high_ref, *outs
):
    grads_ref, scaled_ref = outs
    planes, capacity, wide = tok_ref.shape
    width = wide - LANE
    count = planes * capacity
    units = saved_ref.shape[4]
    tok = tok_ref[...].reshape(count, wide)
    prob = tok[:, width:].astype(F32)
    total = jnp.zeros((count, units), F32)
    far = jnp.concatenate([low_ref[...], high_ref[...]], axis=0)
    for step, down in enumerate((own_ref[...], right_ref[...], far, left_ref[...])):
        owner = lax.rem(place_ref[0] + step, RING)
        z = dot(tok[:, :width], down, ((1,), (1,)))
        a = saved_ref[owner, way, 0].astype(F32)
        b = saved_ref[owner, way, 1].astype(F32)
        sig = jax.nn.sigmoid(a)
        act = a * sig
        total = total + act * b * z
        u = prob * z
        grad_gate = u * b * sig * (1.0 + a * (1.0 - sig))
        grads_ref[:, 2 * step * units : (2 * step + 1) * units] = grad_gate.astype(BF)
        grads_ref[:, (2 * step + 1) * units : (2 * step + 2) * units] = (u * act).astype(BF)
    scaled_ref[...] = jnp.sum(total, axis=1, keepdims=True) * (prob * (1.0 - prob))


def hidden_grads(way, place, tok, saved, down):
    planes, capacity, _ = tok.shape
    count, units = planes * capacity, saved.shape[4]
    whole = pl.BlockSpec(memory_space=pltpu.VMEM)
    return pl.pallas_call(
        functools.partial(hidden_kernel, way),
        in_specs=[pl.BlockSpec(memory_space=pltpu.SMEM)] + [whole] * (2 + len(down)),
        out_shape=[
            jax.ShapeDtypeStruct((count, 2 * RING * units), BF),
            jax.ShapeDtypeStruct((count, LANE), F32),
        ],
        compiler_params=pltpu.CompilerParams(vmem_limit_bytes=VMEM_LIMIT),
        cost_estimate=pl.CostEstimate(
            flops=5 * 10**8, bytes_accessed=5 * 10**6, transcendentals=10**5
        ),
    )(place, tok, saved, *down)


def part_kernel(
    first_ref,
    first_scaled_ref,
    second_ref,
    second_scaled_ref,
    router_ref,
    own_ref,
    left_ref,
    right_ref,
    gate_ref,
    up_ref,
    out_ref,
):
    planes, two, width = out_ref.shape
    capacity = two // 2
    count = planes * capacity
    units = own_ref.shape[2]
    grads = jnp.concatenate([first_ref[...], second_ref[...]], axis=0)
    scaled = jnp.concatenate([first_scaled_ref[...], second_scaled_ref[...]], axis=0)[:, :1]
    block = width // 2
    for part in range(2):
        span = slice(part * block, (part + 1) * block)
        weights = (
            own_ref[0, span],
            own_ref[1, span],
            right_ref[0, span],
            right_ref[1, span],
            gate_ref[span],
            up_ref[span],
            left_ref[0, span],
            left_ref[1, span],
        )
        weights = jnp.concatenate(weights, axis=1)
        total = dot(grads, weights, ((1,), (1,))) + scaled * router_ref[:, span]
        total = total.astype(BF)
        for way in range(2):
            piece = total[way * count : (way + 1) * count].reshape(planes, capacity, block)
            out_ref[:, way * capacity : (way + 1) * capacity, span] = piece


def input_parts(grads, router, weights, capacity):
    (first, first_scaled), (second, second_scaled) = grads
    width = router.shape[1]
    whole = pl.BlockSpec(memory_space=pltpu.VMEM)
    return pl.pallas_call(
        part_kernel,
        in_specs=[whole] * (5 + len(weights)),
        out_shape=jax.ShapeDtypeStruct((first.shape[0] // capacity, 2 * capacity, width), BF),
        compiler_params=pltpu.CompilerParams(vmem_limit_bytes=VMEM_LIMIT),
        cost_estimate=pl.CostEstimate(flops=10**9, bytes_accessed=5 * 10**6, transcendentals=0),
    )(first, first_scaled, second, second_scaled, router, *weights)


def finish_kernel(experts, capacity, routes_ref, first_ref, second_ref, back_ref, *rest):
    out_ref = rest[-1]
    planes, _, width = back_ref.shape
    for way, grad_ref in enumerate((first_ref, second_ref)):
        select = selection(routes_ref[way, 0], planes // experts, capacity, experts).astype(BF)
        back = back_ref[:, way * capacity : (way + 1) * capacity].reshape(planes * capacity, width)
        back = dot(select, back, ((1,), (0,)))
        out_ref[way] = (grad_ref[...].astype(F32) + back).astype(BF)


def finish(part, routes, grads, back, experts, capacity, before):
    tokens, width = grads[0].shape
    block = back.shape[2]
    operands = [routes, *grads, back]
    specs = [
        pl.BlockSpec(routes.shape, lambda i: (0, 0, 0, 0)),
        pl.BlockSpec((tokens, block), lambda i: (0, part)),
        pl.BlockSpec((tokens, block), lambda i: (0, part)),
        pl.BlockSpec(back.shape, lambda i: (0, 0, 0)),
    ]
    aliases = {}
    if before is not None:
        operands.append(before)
        specs.append(pl.BlockSpec(memory_space=pl.ANY))
        aliases = {4: 0}
    return pl.pallas_call(
        functools.partial(finish_kernel, experts, capacity),
        grid=(1,),
        in_specs=specs,
        out_specs=pl.BlockSpec((2, tokens, block), lambda i: (0, 0, part)),
        out_shape=jax.ShapeDtypeStruct((2, tokens, width), BF),
        input_output_aliases=aliases,
        compiler_params=pltpu.CompilerParams(vmem_limit_bytes=VMEM_LIMIT),
        cost_estimate=pl.CostEstimate(flops=10**8, bytes_accessed=3 * 10**6, transcendentals=0),
    )(*operands)


def per_device(pending, routes, probs, saved_gate, saved_up, w_gate, w_up, w_down, w_router):
    members = lax.axis_size("expert")
    experts = w_router.shape[2]
    capacity = pending.shape[2] // experts
    me = lax.axis_index("expert")
    place = lax.rem(me, RING).reshape(1).astype(jnp.int32)
    expert = me // (members // experts)
    along_z, along_x = columns(members), rows(members)

    def exchange(value, groups):
        return lax.all_to_all(
            value, "expert", split_axis=0, concat_axis=0, axis_index_groups=groups, tiled=True
        )

    incoming = (shifted(pending[0, 0], "section", -1), shifted(pending[1, 0], "section", 1))
    saved = exchange(saved_blocks(saved_gate[:, 0, 0], saved_up[:, 0, 0]), along_x)

    width = w_gate.shape[1] // 2
    spans = [slice(part * width, (part + 1) * width) for part in range(2)]
    half = w_down.shape[1] // 2
    own = w_down[0]
    left, right = turned(own, 1), turned(own, RING - 1)
    sent = list(pick(incoming, routes, probs, experts, capacity))
    sent[0], saved, left, right = lax.optimization_barrier((sent[0], saved, left, right))
    down = (own, left, right, turned(left[:half], 1), turned(right[half:], RING - 1))

    own = jnp.stack([w_gate[0, spans[0]], w_up[0, spans[0]]])
    left, right = turned(own, 1), turned(own, RING - 1)
    sent[1], left, right = lax.optimization_barrier((sent[1], left, right))
    weights = [(own, left, right, turned(left[0], 1), turned(right[1], RING - 1))]

    own = jnp.stack([w_gate[0, spans[1]], w_up[0, spans[1]]])
    own, down = lax.optimization_barrier((own, down))
    left, right = turned(own, 1), turned(own, RING - 1)
    weights.append((own, left, right, turned(left[0], 1), turned(right[1], RING - 1)))
    router = lax.dynamic_slice(w_router[0], (0, expert), (2 * width, 1)).reshape(1, 2 * width)

    toks = [exchange(sent[way], along_z) for way in range(2)]
    grads = [hidden_grads(way, place, toks[way], saved, down) for way in range(2)]
    out = None
    for part in range(2):
        parts = input_parts(grads, router[:, spans[part]], weights[part], capacity)
        back = exchange(parts, along_z)
        out = finish(part, routes, incoming, back, experts, capacity, out)
    return out[:, None]


def solution(mesh):
    in_specs = (
        P(None, "section", "expert", None),
        P(None, "section", "expert", None),
        P(None, "section", "expert"),
        P(None, "section", "expert", None, None, None),
        P(None, "section", "expert", None, None, None),
        P("section", None, "expert"),
        P("section", None, "expert"),
        P("section", "expert", None),
        P("section", None, None),
    )
    out_specs = P(None, "section", "expert", None)
    return jax.shard_map(
        per_device, mesh=mesh, in_specs=in_specs, out_specs=out_specs, check_vma=False
    )
```

time: 432 us -> 182 us (0.42)
  the two profiles are of different devices: /device:TPU:10 before, /device:TPU:54 now
where the time goes in v1:
time: 182 us; the launch traced here: 180 us
  starting transfers between devices  74.3 us (41%)
  waiting for transfers between devices  64.1 us (35%)
  local copies, waits for them, and re-layouts  22.7 us (12%)
  Pallas kernels  15.7 us (9%)
  other arithmetic  3.16 us (2%)
    all_to_all x5, starting transfers between devices, exchange(): lax.all_to_all(value, 'expert', split_axis=0, concat_axis=0, axis_index_g...  36.9 us
    ppermute x12, starting transfers between devices, turned(): return lax.ppermute(value, 'expert', pairs)  36.9 us
    ppermute x12, waiting for transfers between devices, turned(): return lax.ppermute(value, 'expert', pairs)  31.8 us
    all_to_all x5, waiting for transfers between devices, exchange(): lax.all_to_all(value, 'expert', split_axis=0, concat_axis=0, axis_index_g...  31.3 us
    unnamed x46, local copies, waits for them, and re-layouts  12.1 us
    pallas_call x2, Pallas kernels, input_parts(): pl.pallas_call(part_kernel, in_specs=[whole] * (5 + len(weights)), out_sh...  7.26 us
    pallas_call x2, Pallas kernels, hidden_grads(): pl.pallas_call(functools.partial(hidden_kernel, way), in_specs=[pl.BlockS...  4.87 us
  transfers between devices with their start and end apart: 19, of which 9 were waited for; matrix products, arithmetic and copies ran while one was open for 8% of the time, Pallas kernels for 8%

profile of v1, /device:TPU:54, one launch (start us, length us, event | category | flops | bytes accessed | tf_op | source)
XLA Modules:
  0.0 180.3 jit_solution(8124160865614716261)
XLA Ops:
  0.0 2.5 %collective-permute-start.2 = (bf16[128,3584]{1,0:T(8,128)(2,1)}, bf16[128,3584]{1,0:T(8,128)(2,1)S(1)}, u32[]{:S(2)}, u32[]{:S(2)}) collective-permute-start(bf16[128,3584]{1,0:T(8,128)(2,1)} %bitcast.21), channel_id=1, source_target_pairs={{0,1},{1,2},{2,3},{3,0},{4,5},{5,6},{6,7},{7,4},{8,9},{9,10},{10,1... | collective-permute-start | bytes 2752520 | tf_op jit(solution)/shard_map/ppermute | solution.py:26
  2.5 3.5 %collective-permute-start.3 = (bf16[128,3584]{1,0:T(8,128)(2,1)}, bf16[128,3584]{1,0:T(8,128)(2,1)S(1)}, u32[]{:S(2)}, u32[]{:S(2)}) collective-permute-start(bf16[128,3584]{1,0:T(8,128)(2,1)} %bitcast.22), channel_id=1, source_target_pairs={{0,3},{1,0},{2,1},{3,2},{4,7},{5,4},{6,5},{7,6},{8,11},{9,8},{10,9... | collective-permute-start | bytes 2752520 | tf_op jit(solution)/shard_map/ppermute | solution.py:26
  6.0 2.2 %slice_bitcast_fusion.4 = (bf16[64,3584]{1,0:T(8,128)(2,1)}, bf16[64,3584]{1,0:T(8,128)(2,1)}) fusion(bf16[2,1,64,3584]{3,2,1,0:T(8,128)(2,1)} %param.9), kind=kLoop, calls=%fused_computation.6 | loop fusion | bytes 1835008 | tf_op jit(solution)/shard_map/squeeze | solution.py:257
  8.2 0.2 collective-permute-start
  8.4 0.3 collective-permute-start.1
  8.7 0.0 copy-start.4
  8.7 0.8 copy-done.4
  9.5 5.3 %all-to-all-start = ((bf16[4,2,2,128,128]{4,3,2,1,0:T(8,128)(2,1)}), bf16[4,2,2,128,128]{4,3,2,1,0:T(8,128)(2,1)S(1)}, u32[]{:S(2)}, u32[]{:S(2)}) async-start(bf16[4,2,2,128,128]{4,3,2,1,0:T(8,128)(2,1)} %copy-done.4), calls=%async_computation | async-start | bytes 1048576 | tf_op jit(solution)/shard_map/all_to_all | solution.py:253
  14.8 0.1 copy.14.routes_ref
  14.9 0.5 copy-done.21
  15.5 0.0 collective-permute-done.rest_0_.first_ref
  15.5 1.1 collective-permute-done.1.rest_1_.second_ref
  16.5 0.8 shard_map.91
  17.4 1.0 copy-done.16
  18.3 0.9 copy-done.17
  19.3 14.0 %all-to-all-done.saved_ref = bf16[4,2,2,128,128]{4,3,2,1,0:T(8,128)(2,1)S(1)} async-done(((bf16[4,2,2,128,128]{4,3,2,1,0:T(8,128)(2,1)}), bf16[4,2,2,128,128]{4,3,2,1,0:T(8,128)(2,1)S(1)}, u32[]{:S(2)}, u32[]{:S(2)}) %all-to-all-start) | async-done | bytes 524320 | tf_op jit(solution)/shard_map/all_to_all | solution.py:253
  33.3 0.0 collective-permute-done.2.left_ref
  33.3 0.0 collective-permute-done.3.right_ref
  33.3 10.3 %all-to-all-start.1 = ((bf16[8,16,3712]{2,1,0:T(8,128)(2,1)}), bf16[8,16,3712]{2,1,0:T(8,128)(2,1)}, u32[]{:S(2)}, u32[]{:S(2)}) async-start(bf16[8,16,3712]{2,1,0:T(8,128)(2,1)} %copy-done.17), calls=%async_computation.1 | async-start | bytes 1900544 | tf_op jit(solution)/shard_map/all_to_all | solution.py:253
  43.6 2.5 %fusion = (bf16[1,1792,128]{2,1,0:T(8,128)(2,1)S(1)}, bf16[1,1792,128]{2,1,0:T(8,128)(2,1)}, bf16[1,1792,128]{2,1,0:T(8,128)(2,1)}, bf16[1,1792,128]{2,1,0:T(8,128)(2,1)S(1)}) fusion(bf16[1,3584,128]{2,1,0:T(8,128)(2,1)} %param.14, bf16[1,3584,128]{2,1,0:T(8,128)(2,1)} %param.15), kind=kLoop, calls=%fused_computation.9 | loop fusion | bytes 3670016 | tf_op jit(solution)/shard_map/slice | solution.py:269
  46.1 1.0 pad_maximum_fusion.1.own_ref
  47.1 1.9 %collective-permute-start.6 = (bf16[2,1792,128]{2,1,0:T(8,128)(2,1)}, bf16[2,1792,128]{2,1,0:T(8,128)(2,1)}, u32[]{:S(2)}, u32[]{:S(2)}) collective-permute-start(bf16[2,1792,128]{2,1,0:T(8,128)(2,1)} %pad_maximum_fusion.1.own_ref), channel_id=1, source_target_pairs={{0,1},{1,2},{2,3},{3,0},{4,5},{5,6},{6,7},{7,4},{8,9},{9,10},{10,1... | collective-permute-start | bytes 2752520 | tf_op jit(solution)/shard_map/ppermute | solution.py:26
  49.0 3.9 %collective-permute-start.7 = (bf16[2,1792,128]{2,1,0:T(8,128)(2,1)}, bf16[2,1792,128]{2,1,0:T(8,128)(2,1)}, u32[]{:S(2)}, u32[]{:S(2)}) collective-permute-start(bf16[2,1792,128]{2,1,0:T(8,128)(2,1)} %pad_maximum_fusion.1.own_ref), channel_id=1, source_target_pairs={{0,3},{1,0},{2,1},{3,2},{4,7},{5,4},{6,5},{7,6},{8,11},{9,8},{10,9... | collective-permute-start | bytes 2752520 | tf_op jit(solution)/shard_map/ppermute | solution.py:26
  53.0 16.3 %collective-permute-done.6.left_ref = bf16[2,1792,128]{2,1,0:T(8,128)(2,1)} collective-permute-done((bf16[2,1792,128]{2,1,0:T(8,128)(2,1)}, bf16[2,1792,128]{2,1,0:T(8,128)(2,1)}, u32[]{:S(2)}, u32[]{:S(2)}) %collective-permute-start.6) | collective-permute-done | bytes 917536 | tf_op jit(solution)/shard_map/ppermute | solution.py:26
  69.4 3.1 %collective-permute-done.7.right_ref = bf16[2,1792,128]{2,1,0:T(8,128)(2,1)} collective-permute-done((bf16[2,1792,128]{2,1,0:T(8,128)(2,1)}, bf16[2,1792,128]{2,1,0:T(8,128)(2,1)}, u32[]{:S(2)}, u32[]{:S(2)}) %collective-permute-start.7) | collective-permute-done | bytes 917536 | tf_op jit(solution)/shard_map/ppermute | solution.py:26
  72.5 0.0 all-to-all-done.1.tok_ref
  72.5 6.9 %all-to-all-start.2 = ((bf16[8,16,3712]{2,1,0:T(8,128)(2,1)}), bf16[8,16,3712]{2,1,0:T(8,128)(2,1)}, u32[]{:S(2)}, u32[]{:S(2)}) async-start(bf16[8,16,3712]{2,1,0:T(8,128)(2,1)} %copy-done.16), calls=%async_computation.2 | async-start | bytes 1900544 | tf_op jit(solution)/shard_map/all_to_all | solution.py:253
  79.4 2.2 %pad_maximum_fusion.own_ref = bf16[2,1792,128]{2,1,0:T(8,128)(2,1)} fusion(bf16[1,1792,128]{2,1,0:T(8,128)(2,1)} %get-tuple-element.51, bf16[1,1792,128]{2,1,0:T(8,128)(2,1)} %get-tuple-element.44), kind=kLoop, calls=%fused_computation | loop fusion | flops 458752 | bytes 1835008 | tf_op jit(solution)/shard_map/stack | solution.py:274
  81.6 3.1 %collective-permute-start.4 = (bf16[64,3584]{1,0:T(8,128)(2,1)S(1)}, bf16[64,3584]{1,0:T(8,128)(2,1)S(1)}, u32[]{:S(2)}, u32[]{:S(2)}) collective-permute-start(bf16[64,3584]{1,0:T(8,128)(2,1)S(1)} %slice.46), channel_id=1, source_target_pairs={{0,1},{1,2},{2,3},{3,0},{4,5},{5,6},{6,7},{7,4},{8,9},{9,10},{10,1... | collective-permute-start | bytes 1376264 | tf_op jit(solution)/shard_map/ppermute | solution.py:26
  84.8 2.8 %collective-permute-start.5 = (bf16[64,3584]{1,0:T(8,128)(2,1)S(1)}, bf16[64,3584]{1,0:T(8,128)(2,1)S(1)}, u32[]{:S(2)}, u32[]{:S(2)}) collective-permute-start(bf16[64,3584]{1,0:T(8,128)(2,1)S(1)} %slice.47), channel_id=1, source_target_pairs={{0,3},{1,0},{2,1},{3,2},{4,7},{5,4},{6,5},{7,6},{8,11},{9,8},{10,9... | collective-permute-start | bytes 1376264 | tf_op jit(solution)/shard_map/ppermute | solution.py:26
  87.5 1.9 %slice_bitcast_fusion.3 = bf16[1792,128]{1,0:T(8,128)(2,1)} fusion(bf16[2,1792,128]{2,1,0:T(8,128)(2,1)} %collective-permute-done.6.left_ref), kind=kLoop, calls=%fused_computation.5 | loop fusion | bytes 917504 | tf_op jit(solution)/shard_map/squeeze | solution.py:272
  89.4 4.3 %collective-permute-start.12 = (bf16[1792,128]{1,0:T(8,128)(2,1)}, bf16[1792,128]{1,0:T(8,128)(2,1)}, u32[]{:S(2)}, u32[]{:S(2)}) collective-permute-start(bf16[1792,128]{1,0:T(8,128)(2,1)} %slice_bitcast_fusion.3), channel_id=1, source_target_pairs={{0,1},{1,2},{2,3},{3,0},{4,5},{5,6},{6,7},{7,4},{8,9},{9,10},{10,1... | collective-permute-start | bytes 1376264 | tf_op jit(solution)/shard_map/ppermute | solution.py:26
  93.7 0.9 collective-permute-done.4.low_ref
  94.6 1.7 collective-permute-done.5.high_ref
  96.3 1.9 %collective-permute-start.8 = (bf16[2,1792,128]{2,1,0:T(8,128)(2,1)}, bf16[2,1792,128]{2,1,0:T(8,128)(2,1)}, u32[]{:S(2)}, u32[]{:S(2)}) collective-permute-start(bf16[2,1792,128]{2,1,0:T(8,128)(2,1)} %pad_maximum_fusion.own_ref), channel_id=1, source_target_pairs={{0,1},{1,2},{2,3},{3,0},{4,5},{5,6},{6,7},{7,4},{8,9},{9,10},{10,1... | collective-permute-start | bytes 2752520 | tf_op jit(solution)/shard_map/ppermute | solution.py:26
  98.3 1.8 %slice_bitcast_fusion.2 = bf16[1792,128]{1,0:T(8,128)(2,1)} fusion(bf16[2,1792,128]{2,1,0:T(8,128)(2,1)} %collective-permute-done.7.right_ref), kind=kLoop, calls=%fused_computation.4 | loop fusion | bytes 917504 | tf_op jit(solution)/shard_map/squeeze | solution.py:272
  100.1 3.9 %collective-permute-start.13 = (bf16[1792,128]{1,0:T(8,128)(2,1)}, bf16[1792,128]{1,0:T(8,128)(2,1)}, u32[]{:S(2)}, u32[]{:S(2)}) collective-permute-start(bf16[1792,128]{1,0:T(8,128)(2,1)} %slice_bitcast_fusion.2), channel_id=1, source_target_pairs={{0,3},{1,0},{2,1},{3,2},{4,7},{5,4},{6,5},{7,6},{8,11},{9,8},{10,9... | collective-permute-start | bytes 1376264 | tf_op jit(solution)/shard_map/ppermute | solution.py:26
  104.0 1.9 %collective-permute-start.9 = (bf16[2,1792,128]{2,1,0:T(8,128)(2,1)}, bf16[2,1792,128]{2,1,0:T(8,128)(2,1)}, u32[]{:S(2)}, u32[]{:S(2)}) collective-permute-start(bf16[2,1792,128]{2,1,0:T(8,128)(2,1)} %pad_maximum_fusion.own_ref), channel_id=1, source_target_pairs={{0,3},{1,0},{2,1},{3,2},{4,7},{5,4},{6,5},{7,6},{8,11},{9,8},{10,9... | collective-permute-start | bytes 2752520 | tf_op jit(solution)/shard_map/ppermute | solution.py:26
  106.0 0.0 copy-start.2
  106.0 1.2 copy-done.2
  107.1 1.0 copy-done.6
  108.2 1.0 copy-done.9
  109.2 2.4 %shard_map.93 = (bf16[128,1024]{1,0:T(8,128)(2,1)S(1)}, f32[128,128]{1,0:T(8,128)S(1)}) custom-call(s32[1]{0:T(128)} %bitcast.2.place_ref, bf16[8,16,3712]{2,1,0:T(8,128)(2,1)} %all-to-all-done.1.tok_ref, bf16[4,2,2,128,128]{4,3,2,1,0:T(8,128)(2,1)S(1)} %all-to-all-done.saved_ref, bf16[128,3584]{1,0:T(8,128)(2,1)S(1)} %bitcast.23, ...), custom_call_target="tpu_custom_call" | custom-call | flops 500000000 | bytes 5000000 | tf_op jit(solution)/shard_map/pallas_call | solution.py:139
  111.6 0.7 copy-done.11
  112.3 0.0 all-to-all-done.2.tok_ref
  112.3 1.2 copy-done.3
  113.5 1.0 copy-done.7
  114.5 1.0 copy-done.10
  115.5 2.5 %shard_map.94 = (bf16[128,1024]{1,0:T(8,128)(2,1)S(1)}, f32[128,128]{1,0:T(8,128)S(1)}) custom-call(s32[1]{0:T(128)} %bitcast.2.place_ref, bf16[8,16,3712]{2,1,0:T(8,128)(2,1)} %all-to-all-done.2.tok_ref, bf16[4,2,2,128,128]{4,3,2,1,0:T(8,128)(2,1)S(1)} %all-to-all-done.saved_ref, bf16[128,3584]{1,0:T(8,128)(2,1)S(1)} %bitcast.24, ...), custom_call_target="tpu_custom_call" | custom-call | flops 500000000 | bytes 5000000 | tf_op jit(solution)/shard_map/pallas_call | solution.py:139
  118.0 4.2 %shard_map.96 = bf16[8,32,1792]{2,1,0:T(8,128)(2,1)} custom-call(bf16[128,1024]{1,0:T(8,128)(2,1)S(1)} %copy-done.12, f32[128,128]{1,0:T(8,128)S(1)} %get-tuple-element.35.first_scaled_ref, bf16[128,1024]{1,0:T(8,128)(2,1)S(1)} %get-tuple-element.38.second_ref, f32[128,128]{1,0:T(8,128)S(1)} %get-tuple-element.39.second_scaled_ref, ...), custom_call_target="tpu_custom_call" | custom-call | flops 1000000000 | bytes 5000000 | tf_op jit(solution)/shard_map/pallas_call | solution.py:197
  122.3 0.7 copy-done.14
  123.0 7.2 %all-to-all-start.4 = ((bf16[8,32,1792]{2,1,0:T(8,128)(2,1)}), bf16[8,32,1792]{2,1,0:T(8,128)(2,1)S(1)}, u32[]{:S(2)}, u32[]{:S(2)}) async-start(bf16[8,32,1792]{2,1,0:T(8,128)(2,1)} %shard_map.96), calls=%async_computation.4 | async-start | bytes 1835008 | tf_op jit(solution)/shard_map/all_to_all | solution.py:253
  130.2 1.0 slice_bitcast_fusion.1
  131.3 5.3 %collective-permute-start.10 = (bf16[1792,128]{1,0:T(8,128)(2,1)S(1)}, bf16[1792,128]{1,0:T(8,128)(2,1)S(1)}, u32[]{:S(2)}, u32[]{:S(2)}) collective-permute-start(bf16[1792,128]{1,0:T(8,128)(2,1)S(1)} %slice_bitcast_fusion.1), channel_id=1, source_target_pairs={{0,1},{1,2},{2,3},{3,0},{4,5},{5,6},{6,7},{7,4},{8,9},{9,10},{10,1... | collective-permute-start | bytes 1376264 | tf_op jit(solution)/shard_map/ppermute | solution.py:26
  136.5 1.1 slice_bitcast_fusion
  137.6 1.9 %collective-permute-start.11 = (bf16[1792,128]{1,0:T(8,128)(2,1)S(1)}, bf16[1792,128]{1,0:T(8,128)(2,1)S(1)}, u32[]{:S(2)}, u32[]{:S(2)}) collective-permute-start(bf16[1792,128]{1,0:T(8,128)(2,1)S(1)} %slice_bitcast_fusion), channel_id=1, source_target_pairs={{0,3},{1,0},{2,1},{3,2},{4,7},{5,4},{6,5},{7,6},{8,11},{9,8},{10,9... | collective-permute-start | bytes 1376264 | tf_op jit(solution)/shard_map/ppermute | solution.py:26
  139.5 3.0 %collective-permute-done.10.gate_ref = bf16[1792,128]{1,0:T(8,128)(2,1)S(1)} collective-permute-done((bf16[1792,128]{1,0:T(8,128)(2,1)S(1)}, bf16[1792,128]{1,0:T(8,128)(2,1)S(1)}, u32[]{:S(2)}, u32[]{:S(2)}) %collective-permute-start.10) | collective-permute-done | bytes 458784 | tf_op jit(solution)/shard_map/ppermute | solution.py:26
  142.5 6.7 %collective-permute-done.11.up_ref = bf16[1792,128]{1,0:T(8,128)(2,1)S(1)} collective-permute-done((bf16[1792,128]{1,0:T(8,128)(2,1)S(1)}, bf16[1792,128]{1,0:T(8,128)(2,1)S(1)}, u32[]{:S(2)}, u32[]{:S(2)}) %collective-permute-start.11) | collective-permute-done | bytes 458784 | tf_op jit(solution)/shard_map/ppermute | solution.py:26
  149.2 3.0 %shard_map.95 = bf16[8,32,1792]{2,1,0:T(8,128)(2,1)S(1)} custom-call(bf16[128,1024]{1,0:T(8,128)(2,1)S(1)} %copy-done.13, f32[128,128]{1,0:T(8,128)S(1)} %get-tuple-element.35.first_scaled_ref, bf16[128,1024]{1,0:T(8,128)(2,1)S(1)} %copy-done.15, f32[128,128]{1,0:T(8,128)S(1)} %get-tuple-element.39.second_scaled_ref, ...), custom_call_target="tpu_custom_call" | custom-call | flops 1000000000 | bytes 5000000 | tf_op jit(solution)/shard_map/pallas_call | solution.py:197
  152.2 0.9 copy-done.1
  153.1 7.2 %all-to-all-start.3 = ((bf16[8,32,1792]{2,1,0:T(8,128)(2,1)}), bf16[8,32,1792]{2,1,0:T(8,128)(2,1)S(1)}, u32[]{:S(2)}, u32[]{:S(2)}) async-start(bf16[8,32,1792]{2,1,0:T(8,128)(2,1)} %copy-done.1), calls=%async_computation.3 | async-start | bytes 1835008 | tf_op jit(solution)/shard_map/all_to_all | solution.py:253
  160.3 1.4 shard_map.97.rest_0_
  161.7 17.2 %all-to-all-done.3.back_ref = bf16[8,32,1792]{2,1,0:T(8,128)(2,1)S(1)} async-done(((bf16[8,32,1792]{2,1,0:T(8,128)(2,1)}), bf16[8,32,1792]{2,1,0:T(8,128)(2,1)S(1)}, u32[]{:S(2)}, u32[]{:S(2)}) %all-to-all-start.3) | async-done | bytes 917536 | tf_op jit(solution)/shard_map/all_to_all | solution.py:253
  178.9 1.4 shard_map.98
  (40 shorter events, 0.2 us)
Async XLA Ops:
  0.0 53.0 %copy-start = (f32[1,3584,4]{1,2,0:T(4,128)S(1)}, f32[1,3584,4]{1,2,0:T(4,128)}, u32[]{:S(2)}) copy-start(f32[1,3584,4]{1,2,0:T(4,128)} %param.17) | copy-start | bytes 172036
  0.0 8.7 %copy-start.18 = (bf16[2,1,1,32,16,128]{5,4,3,2,1,0:T(8,128)(2,1)S(1)}, bf16[2,1,1,32,16,128]{5,4,3,2,1,0:T(8,128)(2,1)}, u32[]{:S(2)}) copy-start(bf16[2,1,1,32,16,128]{5,4,3,2,1,0:T(8,128)(2,1)} %param.12) | copy-start | bytes 786436
  0.0 8.7 %copy-start.19 = (bf16[2,1,1,32,16,128]{5,4,3,2,1,0:T(8,128)(2,1)S(1)}, bf16[2,1,1,32,16,128]{5,4,3,2,1,0:T(8,128)(2,1)}, u32[]{:S(2)}) copy-start(bf16[2,1,1,32,16,128]{5,4,3,2,1,0:T(8,128)(2,1)} %param.13) | copy-start | bytes 786436
  0.0 33.3 %collective-permute-start.2 = (bf16[128,3584]{1,0:T(8,128)(2,1)}, bf16[128,3584]{1,0:T(8,128)(2,1)S(1)}, u32[]{:S(2)}, u32[]{:S(2)}) collective-permute-start(bf16[128,3584]{1,0:T(8,128)(2,1)} %bitcast.21), channel_id=1, source_target_pairs={{0,1},{1,2},{2,3},{3,0},{4,5},{5,6},{6,7},{7,4},{8,9},{9,10},{10,1... | collective-permute-start | bytes 2752520 | tf_op jit(solution)/shard_map/ppermute | solution.py:26
  2.5 30.8 %collective-permute-start.3 = (bf16[128,3584]{1,0:T(8,128)(2,1)}, bf16[128,3584]{1,0:T(8,128)(2,1)S(1)}, u32[]{:S(2)}, u32[]{:S(2)}) collective-permute-start(bf16[128,3584]{1,0:T(8,128)(2,1)} %bitcast.22), channel_id=1, source_target_pairs={{0,3},{1,0},{2,1},{3,2},{4,7},{5,4},{6,5},{7,6},{8,11},{9,8},{10,9... | collective-permute-start | bytes 2752520 | tf_op jit(solution)/shard_map/ppermute | solution.py:26
  8.2 7.3 %collective-permute-start = (bf16[64,3584]{1,0:T(8,128)(2,1)}, bf16[64,3584]{1,0:T(8,128)(2,1)S(1)}, u32[]{:S(2)}, u32[]{:S(2)}) collective-permute-start(bf16[64,3584]{1,0:T(8,128)(2,1)} %get-tuple-element.48), channel_id=1, source_target_pairs={{0,480},{32,0},{64,32},{96,64},{128,96},{160,128},{192,160},{224,1... | collective-permute-start | bytes 1376264 | tf_op jit(solution)/shard_map/ppermute | solution.py:20
  8.4 8.1 %collective-permute-start.1 = (bf16[64,3584]{1,0:T(8,128)(2,1)}, bf16[64,3584]{1,0:T(8,128)(2,1)S(1)}, u32[]{:S(2)}, u32[]{:S(2)}) collective-permute-start(bf16[64,3584]{1,0:T(8,128)(2,1)} %get-tuple-element.47), channel_id=1, source_target_pairs={{0,32},{32,64},{64,96},{96,128},{128,160},{160,192},{192,224},{224... | collective-permute-start | bytes 1376264 | tf_op jit(solution)/shard_map/ppermute | solution.py:20
  8.7 0.8 copy-start.4
  9.5 5.3 %copy-start.20 = (s32[2,1,64,1]{2,3,1,0:T(1,128)S(1)}, s32[2,1,64,1]{2,3,1,0:T(1,128)}, u32[]{:S(2)}) copy-start(s32[2,1,64,1]{2,3,1,0:T(1,128)} %param.10) | copy-start | bytes 1540
  9.5 23.8 %all-to-all-start = ((bf16[4,2,2,128,128]{4,3,2,1,0:T(8,128)(2,1)}), bf16[4,2,2,128,128]{4,3,2,1,0:T(8,128)(2,1)S(1)}, u32[]{:S(2)}, u32[]{:S(2)}) async-start(bf16[4,2,2,128,128]{4,3,2,1,0:T(8,128)(2,1)} %copy-done.4), calls=%async_computation | async-start | bytes 1048576 | tf_op jit(solution)/shard_map/all_to_all | solution.py:253
  14.8 0.7 copy-start.21
  17.4 1.0 copy-start.16
  18.3 0.9 copy-start.17
  33.3 39.2 %all-to-all-start.1 = ((bf16[8,16,3712]{2,1,0:T(8,128)(2,1)}), bf16[8,16,3712]{2,1,0:T(8,128)(2,1)}, u32[]{:S(2)}, u32[]{:S(2)}) async-start(bf16[8,16,3712]{2,1,0:T(8,128)(2,1)} %copy-done.17), calls=%async_computation.1 | async-start | bytes 1900544 | tf_op jit(solution)/shard_map/all_to_all | solution.py:253
  47.1 22.2 %collective-permute-start.6 = (bf16[2,1792,128]{2,1,0:T(8,128)(2,1)}, bf16[2,1792,128]{2,1,0:T(8,128)(2,1)}, u32[]{:S(2)}, u32[]{:S(2)}) collective-permute-start(bf16[2,1792,128]{2,1,0:T(8,128)(2,1)} %pad_maximum_fusion.1.own_ref), channel_id=1, source_target_pairs={{0,1},{1,2},{2,3},{3,0},{4,5},{5,6},{6,7},{7,4},{8,9},{9,10},{10,1... | collective-permute-start | bytes 2752520 | tf_op jit(solution)/shard_map/ppermute | solution.py:26
  49.0 23.5 %collective-permute-start.7 = (bf16[2,1792,128]{2,1,0:T(8,128)(2,1)}, bf16[2,1792,128]{2,1,0:T(8,128)(2,1)}, u32[]{:S(2)}, u32[]{:S(2)}) collective-permute-start(bf16[2,1792,128]{2,1,0:T(8,128)(2,1)} %pad_maximum_fusion.1.own_ref), channel_id=1, source_target_pairs={{0,3},{1,0},{2,1},{3,2},{4,7},{5,4},{6,5},{7,6},{8,11},{9,8},{10,9... | collective-permute-start | bytes 2752520 | tf_op jit(solution)/shard_map/ppermute | solution.py:26
  72.5 39.8 %all-to-all-start.2 = ((bf16[8,16,3712]{2,1,0:T(8,128)(2,1)}), bf16[8,16,3712]{2,1,0:T(8,128)(2,1)}, u32[]{:S(2)}, u32[]{:S(2)}) async-start(bf16[8,16,3712]{2,1,0:T(8,128)(2,1)} %copy-done.16), calls=%async_computation.2 | async-start | bytes 1900544 | tf_op jit(solution)/shard_map/all_to_all | solution.py:253
  81.6 13.0 %collective-permute-start.4 = (bf16[64,3584]{1,0:T(8,128)(2,1)S(1)}, bf16[64,3584]{1,0:T(8,128)(2,1)S(1)}, u32[]{:S(2)}, u32[]{:S(2)}) collective-permute-start(bf16[64,3584]{1,0:T(8,128)(2,1)S(1)} %slice.46), channel_id=1, source_target_pairs={{0,1},{1,2},{2,3},{3,0},{4,5},{5,6},{6,7},{7,4},{8,9},{9,10},{10,1... | collective-permute-start | bytes 1376264 | tf_op jit(solution)/shard_map/ppermute | solution.py:26
  84.8 11.6 %collective-permute-start.5 = (bf16[64,3584]{1,0:T(8,128)(2,1)S(1)}, bf16[64,3584]{1,0:T(8,128)(2,1)S(1)}, u32[]{:S(2)}, u32[]{:S(2)}) collective-permute-start(bf16[64,3584]{1,0:T(8,128)(2,1)S(1)} %slice.47), channel_id=1, source_target_pairs={{0,3},{1,0},{2,1},{3,2},{4,7},{5,4},{6,5},{7,6},{8,11},{9,8},{10,9... | collective-permute-start | bytes 1376264 | tf_op jit(solution)/shard_map/ppermute | solution.py:26
  89.4 28.6 %collective-permute-start.12 = (bf16[1792,128]{1,0:T(8,128)(2,1)}, bf16[1792,128]{1,0:T(8,128)(2,1)}, u32[]{:S(2)}, u32[]{:S(2)}) collective-permute-start(bf16[1792,128]{1,0:T(8,128)(2,1)} %slice_bitcast_fusion.3), channel_id=1, source_target_pairs={{0,1},{1,2},{2,3},{3,0},{4,5},{5,6},{6,7},{7,4},{8,9},{9,10},{10,1... | collective-permute-start | bytes 1376264 | tf_op jit(solution)/shard_map/ppermute | solution.py:26
  94.6 5.5 %copy-start.5 = (bf16[64,3584]{1,0:T(8,128)(2,1)}, bf16[64,3584]{1,0:T(8,128)(2,1)S(1)}, u32[]{:S(2)}) copy-start(bf16[64,3584]{1,0:T(8,128)(2,1)S(1)} %collective-permute-done.4.low_ref) | copy-start | bytes 1376260
  96.3 3.8 %copy-start.8 = (bf16[64,3584]{1,0:T(8,128)(2,1)}, bf16[64,3584]{1,0:T(8,128)(2,1)S(1)}, u32[]{:S(2)}) copy-start(bf16[64,3584]{1,0:T(8,128)(2,1)S(1)} %collective-permute-done.5.high_ref) | copy-start | bytes 1376260
  96.3 33.8 %collective-permute-start.8 = (bf16[2,1792,128]{2,1,0:T(8,128)(2,1)}, bf16[2,1792,128]{2,1,0:T(8,128)(2,1)}, u32[]{:S(2)}, u32[]{:S(2)}) collective-permute-start(bf16[2,1792,128]{2,1,0:T(8,128)(2,1)} %pad_maximum_fusion.own_ref), channel_id=1, source_target_pairs={{0,1},{1,2},{2,3},{3,0},{4,5},{5,6},{6,7},{7,4},{8,9},{9,10},{10,1... | collective-permute-start | bytes 2752520 | tf_op jit(solution)/shard_map/ppermute | solution.py:26
  100.1 17.9 %collective-permute-start.13 = (bf16[1792,128]{1,0:T(8,128)(2,1)}, bf16[1792,128]{1,0:T(8,128)(2,1)}, u32[]{:S(2)}, u32[]{:S(2)}) collective-permute-start(bf16[1792,128]{1,0:T(8,128)(2,1)} %slice_bitcast_fusion.2), channel_id=1, source_target_pairs={{0,3},{1,0},{2,1},{3,2},{4,7},{5,4},{6,5},{7,6},{8,11},{9,8},{10,9... | collective-permute-start | bytes 1376264 | tf_op jit(solution)/shard_map/ppermute | solution.py:26
  104.0 32.5 %collective-permute-start.9 = (bf16[2,1792,128]{2,1,0:T(8,128)(2,1)}, bf16[2,1792,128]{2,1,0:T(8,128)(2,1)}, u32[]{:S(2)}, u32[]{:S(2)}) collective-permute-start(bf16[2,1792,128]{2,1,0:T(8,128)(2,1)} %pad_maximum_fusion.own_ref), channel_id=1, source_target_pairs={{0,3},{1,0},{2,1},{3,2},{4,7},{5,4},{6,5},{7,6},{8,11},{9,8},{10,9... | collective-permute-start | bytes 2752520 | tf_op jit(solution)/shard_map/ppermute | solution.py:26
  106.0 1.2 copy-start.2
  107.1 1.0 copy-start.6
  108.2 1.0 copy-start.9
  111.6 0.7 copy-start.11
  112.3 1.2 copy-start.3
  113.5 1.0 copy-start.7
  114.5 1.0 copy-start.10
  115.5 2.5 %copy-start.12 = (bf16[128,1024]{1,0:T(8,128)(2,1)S(1)}, bf16[128,1024]{1,0:T(8,128)(2,1)}, u32[]{:S(2)}) copy-start(bf16[128,1024]{1,0:T(8,128)(2,1)} %copy-done.11) | copy-start | bytes 786436
  122.2 0.7 copy-start.14
  123.0 30.2 %all-to-all-start.4 = ((bf16[8,32,1792]{2,1,0:T(8,128)(2,1)}), bf16[8,32,1792]{2,1,0:T(8,128)(2,1)S(1)}, u32[]{:S(2)}, u32[]{:S(2)}) async-start(bf16[8,32,1792]{2,1,0:T(8,128)(2,1)} %shard_map.96), calls=%async_computation.4 | async-start | bytes 1835008 | tf_op jit(solution)/shard_map/all_to_all | solution.py:253
  131.2 17.9 %copy-start.13 = (bf16[128,1024]{1,0:T(8,128)(2,1)S(1)}, bf16[128,1024]{1,0:T(8,128)(2,1)}, u32[]{:S(2)}) copy-start(bf16[128,1024]{1,0:T(8,128)(2,1)} %copy-done.11) | copy-start | bytes 786436
  131.2 17.9 %copy-start.15 = (bf16[128,1024]{1,0:T(8,128)(2,1)S(1)}, bf16[128,1024]{1,0:T(8,128)(2,1)}, u32[]{:S(2)}) copy-start(bf16[128,1024]{1,0:T(8,128)(2,1)} %copy-done.14) | copy-start | bytes 786436
  131.3 11.2 %collective-permute-start.10 = (bf16[1792,128]{1,0:T(8,128)(2,1)S(1)}, bf16[1792,128]{1,0:T(8,128)(2,1)S(1)}, u32[]{:S(2)}, u32[]{:S(2)}) collective-permute-start(bf16[1792,128]{1,0:T(8,128)(2,1)S(1)} %slice_bitcast_fusion.1), channel_id=1, source_target_pairs={{0,1},{1,2},{2,3},{3,0},{4,5},{5,6},{6,7},{7,4},{8,9},{9,10},{10,1... | collective-permute-start | bytes 1376264 | tf_op jit(solution)/shard_map/ppermute | solution.py:26
  137.6 11.6 %collective-permute-start.11 = (bf16[1792,128]{1,0:T(8,128)(2,1)S(1)}, bf16[1792,128]{1,0:T(8,128)(2,1)S(1)}, u32[]{:S(2)}, u32[]{:S(2)}) collective-permute-start(bf16[1792,128]{1,0:T(8,128)(2,1)S(1)} %slice_bitcast_fusion), channel_id=1, source_target_pairs={{0,3},{1,0},{2,1},{3,2},{4,7},{5,4},{6,5},{7,6},{8,11},{9,8},{10,9... | collective-permute-start | bytes 1376264 | tf_op jit(solution)/shard_map/ppermute | solution.py:26
  152.2 0.9 copy-start.1
  153.1 25.8 %all-to-all-start.3 = ((bf16[8,32,1792]{2,1,0:T(8,128)(2,1)}), bf16[8,32,1792]{2,1,0:T(8,128)(2,1)S(1)}, u32[]{:S(2)}, u32[]{:S(2)}) async-start(bf16[8,32,1792]{2,1,0:T(8,128)(2,1)} %copy-done.1), calls=%async_computation.3 | async-start | bytes 1835008 | tf_op jit(solution)/shard_map/all_to_all | solution.py:253

commit v2 on v1

--- a/solution.py
+++ b/solution.py
@@ -10,6 +10,7 @@
 BF = jnp.bfloat16
 F32 = jnp.float32
 LANE = 128
+FLOPS = (10000000000, 1000000000)
 RING = 4
 VMEM_LIMIT = 48 * 1024 * 1024
 
@@ -145,7 +146,7 @@
         ],
         compiler_params=pltpu.CompilerParams(vmem_limit_bytes=VMEM_LIMIT),
         cost_estimate=pl.CostEstimate(
-            flops=5 * 10**8, bytes_accessed=5 * 10**6, transcendentals=10**5
+            flops=10000000000, bytes_accessed=5 * 10**6, transcendentals=10**5
         ),
     )(place, tok, saved, *down)
 
@@ -190,7 +191,7 @@
             out_ref[:, way * capacity : (way + 1) * capacity, span] = piece
 
 
-def input_parts(grads, router, weights, capacity):
+def input_parts(flops, grads, router, weights, capacity):
     (first, first_scaled), (second, second_scaled) = grads
     width = router.shape[1]
     whole = pl.BlockSpec(memory_space=pltpu.VMEM)
@@ -199,7 +200,7 @@
         in_specs=[whole] * (5 + len(weights)),
         out_shape=jax.ShapeDtypeStruct((first.shape[0] // capacity, 2 * capacity, width), BF),
         compiler_params=pltpu.CompilerParams(vmem_limit_bytes=VMEM_LIMIT),
-        cost_estimate=pl.CostEstimate(flops=10**9, bytes_accessed=5 * 10**6, transcendentals=0),
+        cost_estimate=pl.CostEstimate(flops=flops, bytes_accessed=5 * 10**6, transcendentals=0),
     )(first, first_scaled, second, second_scaled, router, *weights)
 
 
@@ -260,28 +261,33 @@
     width = w_gate.shape[1] // 2
     spans = [slice(part * width, (part + 1) * width) for part in range(2)]
     half = w_down.shape[1] // 2
+    sent = list(pick(incoming, routes, probs, experts, capacity))
     own = w_down[0]
-    left, right = turned(own, 1), turned(own, RING - 1)
-    sent = list(pick(incoming, routes, probs, experts, capacity))
-    sent[0], saved, left, right = lax.optimization_barrier((sent[0], saved, left, right))
-    down = (own, left, right, turned(left[:half], 1), turned(right[half:], RING - 1))
-
+    wl, wr = turned(own, 1), turned(own, RING - 1)
+    wf, wg = turned(wl[:half], 1), turned(wr[half:], RING - 1)
+    down = (own, wl, wr, wf, wg)
     own = jnp.stack([w_gate[0, spans[0]], w_up[0, spans[0]]])
-    left, right = turned(own, 1), turned(own, RING - 1)
-    sent[1], left, right = lax.optimization_barrier((sent[1], left, right))
-    weights = [(own, left, right, turned(left[0], 1), turned(right[1], RING - 1))]
-
+
+    al, ar = turned(own, 1), turned(own, RING - 1)
+    af, ag = turned(al[0], 1), turned(ar[1], RING - 1)
+    weights = [(own, al, ar, af, ag)]
     own = jnp.stack([w_gate[0, spans[1]], w_up[0, spans[1]]])
-    own, down = lax.optimization_barrier((own, down))
-    left, right = turned(own, 1), turned(own, RING - 1)
-    weights.append((own, left, right, turned(left[0], 1), turned(right[1], RING - 1)))
+    own, _, _, _, _ = lax.optimization_barrier((own, al, ar, wf, wg))
+    bl, br = turned(own, 1), turned(own, RING - 1)
+    bf, bg = turned(bl[0], 1), turned(br[1], RING - 1)
+    weights.append((own, bl, br, bf, bg))
     router = lax.dynamic_slice(w_router[0], (0, expert), (2 * width, 1)).reshape(1, 2 * width)
 
+    sent[0], saved = lax.optimization_barrier((sent[0], saved))
+
+    sent[1], _, _ = lax.optimization_barrier((sent[1], wl, wr))
     toks = [exchange(sent[way], along_z) for way in range(2)]
+
+
     grads = [hidden_grads(way, place, toks[way], saved, down) for way in range(2)]
     out = None
     for part in range(2):
-        parts = input_parts(grads, router[:, spans[part]], weights[part], capacity)
+        parts = input_parts(FLOPS[part], grads, router[:, spans[part]], weights[part], capacity)
         back = exchange(parts, along_z)
         out = finish(part, routes, incoming, back, experts, capacity, out)
     return out[:, None]

time: 182 us -> 159 us (0.87)
  the two profiles are of different devices: /device:TPU:54 before, /device:TPU:31 now
where the time goes in v2:
time: 159 us; the launch traced here: 158 us
  starting transfers between devices  66.7 us (42%)
  waiting for transfers between devices  54.2 us (34%)
  Pallas kernels  18.1 us (11%)
  local copies, waits for them, and re-layouts  17.3 us (11%)
    all_to_all x5, waiting for transfers between devices, exchange(): lax.all_to_all(value, 'expert', split_axis=0, concat_axis=0, axis_index_g...  42.4 us
    ppermute x12, starting transfers between devices, turned(): return lax.ppermute(value, 'expert', pairs)  32.6 us
    all_to_all x5, starting transfers between devices, exchange(): lax.all_to_all(value, 'expert', split_axis=0, concat_axis=0, axis_index_g...  30.9 us
    ppermute x12, waiting for transfers between devices, turned(): return lax.ppermute(value, 'expert', pairs)  11.8 us
    pallas_call x2, Pallas kernels, hidden_grads(): pl.pallas_call(functools.partial(hidden_kernel, way), in_specs=[pl.BlockS...  6.76 us
    pallas_call x2, Pallas kernels, input_parts(): pl.pallas_call(part_kernel, in_specs=[whole] * (5 + len(weights)), out_sh...  6.02 us
    unnamed x32, local copies, waits for them, and re-layouts  4.98 us
    slice x2, local copies, waits for them, and re-layouts, per_device(): wf, wg = (turned(wl[:half], 1), turned(wr[half:], RING - 1))  3.66 us
  transfers between devices with their start and end apart: 19, of which 9 were waited for; matrix products, arithmetic and copies ran while one was open for 8% of the time, Pallas kernels for 11%

profile of v2, /device:TPU:31, one launch (start us, length us, event | category | flops | bytes accessed | tf_op | source)
XLA Modules:
  0.0 157.7 jit_solution(13012162656736173337)
XLA Ops:
  0.0 1.3 slice_bitcast_fusion.4
  1.3 0.7 collective-permute-start
  2.0 2.4 %collective-permute-start.1 = (bf16[64,3584]{1,0:T(8,128)(2,1)S(1)}, bf16[64,3584]{1,0:T(8,128)(2,1)S(1)}, u32[]{:S(2)}, u32[]{:S(2)}) collective-permute-start(bf16[64,3584]{1,0:T(8,128)(2,1)S(1)} %get-tuple-element.29), channel_id=1, source_target_pairs={{0,32},{32,64},{64,96},{96,128},{128,160},{160,192},{192,224},{224... | collective-permute-start | bytes 1376264 | tf_op jit(solution)/shard_map/ppermute | solution.py:21
  4.4 0.8 shard_map.92
  5.2 4.2 %all-to-all-start = ((bf16[4,2,2,128,128]{4,3,2,1,0:T(8,128)(2,1)}), bf16[4,2,2,128,128]{4,3,2,1,0:T(8,128)(2,1)S(1)}, u32[]{:S(2)}, u32[]{:S(2)}) async-start(bf16[4,2,2,128,128]{4,3,2,1,0:T(8,128)(2,1)} %shard_map.92), calls=%async_computation | async-start | bytes 1048576 | tf_op jit(solution)/shard_map/all_to_all | solution.py:254
  9.4 2.0 %collective-permute-start.2 = (bf16[128,3584]{1,0:T(8,128)(2,1)}, bf16[128,3584]{1,0:T(8,128)(2,1)}, u32[]{:S(2)}, u32[]{:S(2)}) collective-permute-start(bf16[128,3584]{1,0:T(8,128)(2,1)} %bitcast.5.own_ref), channel_id=1, source_target_pairs={{0,1},{1,2},{2,3},{3,0},{4,5},{5,6},{6,7},{7,4},{8,9},{9,10},{10,1... | collective-permute-start | bytes 2752520 | tf_op jit(solution)/shard_map/ppermute | solution.py:27
  11.5 3.4 %collective-permute-start.3 = (bf16[128,3584]{1,0:T(8,128)(2,1)}, bf16[128,3584]{1,0:T(8,128)(2,1)}, u32[]{:S(2)}, u32[]{:S(2)}) collective-permute-start(bf16[128,3584]{1,0:T(8,128)(2,1)} %bitcast.5.own_ref), channel_id=1, source_target_pairs={{0,3},{1,0},{2,1},{3,2},{4,7},{5,4},{6,5},{7,6},{8,11},{9,8},{10,9... | collective-permute-start | bytes 2752520 | tf_op jit(solution)/shard_map/ppermute | solution.py:27
  14.9 0.1 copy.14.routes_ref
  15.0 0.0 collective-permute-done.rest_0_.first_ref
  15.0 0.0 collective-permute-done.1.rest_1_.second_ref
  15.0 1.8 %shard_map.91 = (bf16[8,16,3712]{2,1,0:T(8,128)(2,1)S(1)}, bf16[8,16,3712]{2,1,0:T(8,128)(2,1)}) custom-call(s32[2,1,64,1]{3,2,1,0:T(8,128)S(1)} %copy.14.routes_ref, bf16[2,1,64]{2,1,0:T(2,128)(2,1)S(1)} %copy.12.probs_ref, bf16[64,3584]{1,0:T(8,128)(2,1)S(1)} %collective-permute-done.rest_0_.first_ref, ...), custom_call_target="tpu_custom_call" | custom-call | flops 100000000 | bytes 4000000 | tf_op jit(solution)/shard_map/pallas_call | solution.py:80
  16.8 0.9 copy-done.2
  17.8 0.0 all-to-all-done.saved_ref
  17.8 10.0 %all-to-all-start.1 = ((bf16[8,16,3712]{2,1,0:T(8,128)(2,1)}), bf16[8,16,3712]{2,1,0:T(8,128)(2,1)S(1)}, u32[]{:S(2)}, u32[]{:S(2)}) async-start(bf16[8,16,3712]{2,1,0:T(8,128)(2,1)} %copy-done.2), calls=%async_computation.1 | async-start | bytes 1900544 | tf_op jit(solution)/shard_map/all_to_all | solution.py:254
  27.8 1.6 fusion
  29.4 1.0 pad_maximum_fusion.1.own_ref
  30.4 3.3 %collective-permute-start.6 = (bf16[2,1792,128]{2,1,0:T(8,128)(2,1)}, bf16[2,1792,128]{2,1,0:T(8,128)(2,1)}, u32[]{:S(2)}, u32[]{:S(2)}) collective-permute-start(bf16[2,1792,128]{2,1,0:T(8,128)(2,1)} %pad_maximum_fusion.1.own_ref), channel_id=1, source_target_pairs={{0,1},{1,2},{2,3},{3,0},{4,5},{5,6},{6,7},{7,4},{8,9},{9,10},{10,1... | collective-permute-start | bytes 2752520 | tf_op jit(solution)/shard_map/ppermute | solution.py:27
  33.7 1.9 %collective-permute-start.7 = (bf16[2,1792,128]{2,1,0:T(8,128)(2,1)}, bf16[2,1792,128]{2,1,0:T(8,128)(2,1)}, u32[]{:S(2)}, u32[]{:S(2)}) collective-permute-start(bf16[2,1792,128]{2,1,0:T(8,128)(2,1)} %pad_maximum_fusion.1.own_ref), channel_id=1, source_target_pairs={{0,3},{1,0},{2,1},{3,2},{4,7},{5,4},{6,5},{7,6},{8,11},{9,8},{10,9... | collective-permute-start | bytes 2752520 | tf_op jit(solution)/shard_map/ppermute | solution.py:27
  35.7 0.1 pad_maximum_fusion.own_ref
  35.8 0.3 collective-permute-done.2.left_ref
  36.1 0.2 collective-permute-done.3.right_ref
  36.3 1.8 %slice.56 = bf16[64,3584]{1,0:T(8,128)(2,1)} slice(bf16[128,3584]{1,0:T(8,128)(2,1)} %collective-permute-done.2.left_ref), slice={[0:64], [0:3584]} | slice | bytes 917504 | tf_op jit(solution)/shard_map/slice | solution.py:267
  38.1 4.1 %collective-permute-start.4 = (bf16[64,3584]{1,0:T(8,128)(2,1)}, bf16[64,3584]{1,0:T(8,128)(2,1)}, u32[]{:S(2)}, u32[]{:S(2)}) collective-permute-start(bf16[64,3584]{1,0:T(8,128)(2,1)} %slice.56), channel_id=1, source_target_pairs={{0,1},{1,2},{2,3},{3,0},{4,5},{5,6},{6,7},{7,4},{8,9},{9,10},{10,1... | collective-permute-start | bytes 1376264 | tf_op jit(solution)/shard_map/ppermute | solution.py:27
  42.2 1.8 %slice.57 = bf16[64,3584]{1,0:T(8,128)(2,1)} slice(bf16[128,3584]{1,0:T(8,128)(2,1)} %collective-permute-done.3.right_ref), slice={[64:128], [0:3584]} | slice | bytes 917504 | tf_op jit(solution)/shard_map/slice | solution.py:267
  44.1 1.9 %collective-permute-start.5 = (bf16[64,3584]{1,0:T(8,128)(2,1)}, bf16[64,3584]{1,0:T(8,128)(2,1)}, u32[]{:S(2)}, u32[]{:S(2)}) collective-permute-start(bf16[64,3584]{1,0:T(8,128)(2,1)} %slice.57), channel_id=1, source_target_pairs={{0,3},{1,0},{2,1},{3,2},{4,7},{5,4},{6,5},{7,6},{8,11},{9,8},{10,9... | collective-permute-start | bytes 1376264 | tf_op jit(solution)/shard_map/ppermute | solution.py:27
  46.0 9.0 %all-to-all-done.1.tok_ref = bf16[8,16,3712]{2,1,0:T(8,128)(2,1)S(1)} async-done(((bf16[8,16,3712]{2,1,0:T(8,128)(2,1)}), bf16[8,16,3712]{2,1,0:T(8,128)(2,1)S(1)}, u32[]{:S(2)}, u32[]{:S(2)}) %all-to-all-start.1) | async-done | bytes 950304 | tf_op jit(solution)/shard_map/all_to_all | solution.py:254
  55.0 4.2 %all-to-all-start.2 = ((bf16[8,16,3712]{2,1,0:T(8,128)(2,1)}), bf16[8,16,3712]{2,1,0:T(8,128)(2,1)}, u32[]{:S(2)}, u32[]{:S(2)}) async-start(bf16[8,16,3712]{2,1,0:T(8,128)(2,1)} %get-tuple-element.21), calls=%async_computation.2 | async-start | bytes 1900544 | tf_op jit(solution)/shard_map/all_to_all | solution.py:254
  59.2 0.0 collective-permute-done.6.left_ref
  59.2 1.8 %slice_bitcast_fusion.1 = bf16[1792,128]{1,0:T(8,128)(2,1)} fusion(bf16[2,1792,128]{2,1,0:T(8,128)(2,1)} %collective-permute-done.6.left_ref), kind=kLoop, calls=%fused_computation.3 | loop fusion | bytes 917504 | tf_op jit(solution)/shard_map/squeeze | solution.py:272
  61.1 2.8 %collective-permute-start.12 = (bf16[1792,128]{1,0:T(8,128)(2,1)}, bf16[1792,128]{1,0:T(8,128)(2,1)}, u32[]{:S(2)}, u32[]{:S(2)}) collective-permute-start(bf16[1792,128]{1,0:T(8,128)(2,1)} %slice_bitcast_fusion.1), channel_id=1, source_target_pairs={{0,1},{1,2},{2,3},{3,0},{4,5},{5,6},{6,7},{7,4},{8,9},{9,10},{10,1... | collective-permute-start | bytes 1376264 | tf_op jit(solution)/shard_map/ppermute | solution.py:27
  63.8 0.0 collective-permute-done.7.right_ref
  63.8 1.8 %slice_bitcast_fusion = bf16[1792,128]{1,0:T(8,128)(2,1)} fusion(bf16[2,1792,128]{2,1,0:T(8,128)(2,1)} %collective-permute-done.7.right_ref), kind=kLoop, calls=%fused_computation.2 | loop fusion | bytes 917504 | tf_op jit(solution)/shard_map/squeeze | solution.py:272
  65.7 2.5 %collective-permute-start.13 = (bf16[1792,128]{1,0:T(8,128)(2,1)}, bf16[1792,128]{1,0:T(8,128)(2,1)}, u32[]{:S(2)}, u32[]{:S(2)}) collective-permute-start(bf16[1792,128]{1,0:T(8,128)(2,1)} %slice_bitcast_fusion), channel_id=1, source_target_pairs={{0,3},{1,0},{2,1},{3,2},{4,7},{5,4},{6,5},{7,6},{8,11},{9,8},{10,9... | collective-permute-start | bytes 1376264 | tf_op jit(solution)/shard_map/ppermute | solution.py:27
  68.2 0.0 collective-permute-done.4.low_ref
  68.2 0.9 collective-permute-done.5.high_ref
  69.1 3.1 %collective-permute-start.8 = (bf16[2,1792,128]{2,1,0:T(8,128)(2,1)S(1)}, bf16[2,1792,128]{2,1,0:T(8,128)(2,1)}, u32[]{:S(2)}, u32[]{:S(2)}) collective-permute-start(bf16[2,1792,128]{2,1,0:T(8,128)(2,1)S(1)} %pad_maximum_fusion.own_ref), channel_id=1, source_target_pairs={{0,1},{1,2},{2,3},{3,0},{4,5},{5,6},{6,7},{7,4},{8,9},{9,10},{10,1... | collective-permute-start | bytes 2752520 | tf_op jit(solution)/shard_map/ppermute | solution.py:27
  72.2 2.2 %collective-permute-start.9 = (bf16[2,1792,128]{2,1,0:T(8,128)(2,1)S(1)}, bf16[2,1792,128]{2,1,0:T(8,128)(2,1)}, u32[]{:S(2)}, u32[]{:S(2)}) collective-permute-start(bf16[2,1792,128]{2,1,0:T(8,128)(2,1)S(1)} %pad_maximum_fusion.own_ref), channel_id=1, source_target_pairs={{0,3},{1,0},{2,1},{3,2},{4,7},{5,4},{6,5},{7,6},{8,11},{9,8},{10,9... | collective-permute-start | bytes 2752520 | tf_op jit(solution)/shard_map/ppermute | solution.py:27
  74.4 3.2 %shard_map.93 = (bf16[128,1024]{1,0:T(8,128)(2,1)S(1)}, f32[128,128]{1,0:T(8,128)S(1)}) custom-call(s32[1]{0:T(128)} %bitcast.2.place_ref, bf16[8,16,3712]{2,1,0:T(8,128)(2,1)S(1)} %all-to-all-done.1.tok_ref, bf16[4,2,2,128,128]{4,3,2,1,0:T(8,128)(2,1)S(1)} %all-to-all-done.saved_ref, bf16[128,3584]{1,0:T(8,128)(2,1)} %bitcast.5.own_ref, ...), custom_call_target="tpu_custom_call" | custom-call | flops 10000000000 | bytes 5000000 | tf_op jit(solution)/shard_map/pallas_call | solution.py:140
  77.6 0.7 copy-done.4
  78.3 5.8 %all-to-all-done.2.tok_ref = bf16[8,16,3712]{2,1,0:T(8,128)(2,1)} async-done(((bf16[8,16,3712]{2,1,0:T(8,128)(2,1)}), bf16[8,16,3712]{2,1,0:T(8,128)(2,1)}, u32[]{:S(2)}, u32[]{:S(2)}) %all-to-all-start.2) | async-done | bytes 950304 | tf_op jit(solution)/shard_map/all_to_all | solution.py:254
  84.1 3.5 %shard_map.94 = (bf16[128,1024]{1,0:T(8,128)(2,1)S(1)}, f32[128,128]{1,0:T(8,128)S(1)}) custom-call(s32[1]{0:T(128)} %bitcast.2.place_ref, bf16[8,16,3712]{2,1,0:T(8,128)(2,1)} %all-to-all-done.2.tok_ref, bf16[4,2,2,128,128]{4,3,2,1,0:T(8,128)(2,1)S(1)} %all-to-all-done.saved_ref, bf16[128,3584]{1,0:T(8,128)(2,1)} %bitcast.5.own_ref, ...), custom_call_target="tpu_custom_call" | custom-call | flops 10000000000 | bytes 5000000 | tf_op jit(solution)/shard_map/pallas_call | solution.py:140
  87.7 0.0 collective-permute-done.12.gate_ref
  87.7 0.0 collective-permute-done.13.up_ref
  87.7 3.3 %shard_map.96 = bf16[8,32,1792]{2,1,0:T(8,128)(2,1)S(1)} custom-call(bf16[128,1024]{1,0:T(8,128)(2,1)S(1)} %copy-done.5, f32[128,128]{1,0:T(8,128)S(1)} %get-tuple-element.19.first_scaled_ref, bf16[128,1024]{1,0:T(8,128)(2,1)S(1)} %get-tuple-element.22.second_ref, f32[128,128]{1,0:T(8,128)S(1)} %get-tuple-element.23.second_scaled_ref, ...), custom_call_target="tpu_custom_call" | custom-call | flops 10000000000 | bytes 5000000 | tf_op jit(solution)/shard_map/pallas_call | solution.py:198
  91.0 0.0 copy-start.3
  91.0 0.9 copy-done.3
  91.9 0.7 copy-done.7
  92.6 0.6 copy-done.11
  93.3 3.6 %all-to-all-start.4 = ((bf16[8,32,1792]{2,1,0:T(8,128)(2,1)}), bf16[8,32,1792]{2,1,0:T(8,128)(2,1)S(1)}, u32[]{:S(2)}, u32[]{:S(2)}) async-start(bf16[8,32,1792]{2,1,0:T(8,128)(2,1)} %copy-done.3), calls=%async_computation.4 | async-start | bytes 1835008 | tf_op jit(solution)/shard_map/all_to_all | solution.py:254
  96.8 0.0 collective-permute-done.8.left_ref
  96.8 1.0 slice_bitcast_fusion.3
  97.9 3.3 %collective-permute-start.10 = (bf16[1792,128]{1,0:T(8,128)(2,1)S(1)}, bf16[1792,128]{1,0:T(8,128)(2,1)S(1)}, u32[]{:S(2)}, u32[]{:S(2)}) collective-permute-start(bf16[1792,128]{1,0:T(8,128)(2,1)S(1)} %slice_bitcast_fusion.3), channel_id=1, source_target_pairs={{0,1},{1,2},{2,3},{3,0},{4,5},{5,6},{6,7},{7,4},{8,9},{9,10},{10,1... | collective-permute-start | bytes 1376264 | tf_op jit(solution)/shard_map/ppermute | solution.py:27
  101.2 0.0 collective-permute-done.9.right_ref
  101.2 1.1 slice_bitcast_fusion.2
  102.3 2.1 %collective-permute-start.11 = (bf16[1792,128]{1,0:T(8,128)(2,1)S(1)}, bf16[1792,128]{1,0:T(8,128)(2,1)S(1)}, u32[]{:S(2)}, u32[]{:S(2)}) collective-permute-start(bf16[1792,128]{1,0:T(8,128)(2,1)S(1)} %slice_bitcast_fusion.2), channel_id=1, source_target_pairs={{0,3},{1,0},{2,1},{3,2},{4,7},{5,4},{6,5},{7,6},{8,11},{9,8},{10,9... | collective-permute-start | bytes 1376264 | tf_op jit(solution)/shard_map/ppermute | solution.py:27
  104.4 4.9 %collective-permute-done.10.gate_ref = bf16[1792,128]{1,0:T(8,128)(2,1)S(1)} collective-permute-done((bf16[1792,128]{1,0:T(8,128)(2,1)S(1)}, bf16[1792,128]{1,0:T(8,128)(2,1)S(1)}, u32[]{:S(2)}, u32[]{:S(2)}) %collective-permute-start.10) | collective-permute-done | bytes 458784 | tf_op jit(solution)/shard_map/ppermute | solution.py:27
  109.3 5.6 %collective-permute-done.11.up_ref = bf16[1792,128]{1,0:T(8,128)(2,1)S(1)} collective-permute-done((bf16[1792,128]{1,0:T(8,128)(2,1)S(1)}, bf16[1792,128]{1,0:T(8,128)(2,1)S(1)}, u32[]{:S(2)}, u32[]{:S(2)}) %collective-permute-start.11) | collective-permute-done | bytes 458784 | tf_op jit(solution)/shard_map/ppermute | solution.py:27
  114.9 2.7 %shard_map.95 = bf16[8,32,1792]{2,1,0:T(8,128)(2,1)S(1)} custom-call(bf16[128,1024]{1,0:T(8,128)(2,1)S(1)} %copy-done.6, f32[128,128]{1,0:T(8,128)S(1)} %get-tuple-element.19.first_scaled_ref, bf16[128,1024]{1,0:T(8,128)(2,1)S(1)} %copy-done.8, f32[128,128]{1,0:T(8,128)S(1)} %copy-done.12, f32[1,1792]{1,0:T(1,128)S(1)} %get-tuple-element.32.router_ref, ...), custom_call_target="tpu_custom_call" | custom-call | flops 1000000000 | bytes 5000000 | tf_op jit(solution)/shard_map/pallas_call | solution.py:198
  117.6 0.9 copy-done.1
  118.6 2.5 %all-to-all-done.4.back_ref = bf16[8,32,1792]{2,1,0:T(8,128)(2,1)S(1)} async-done(((bf16[8,32,1792]{2,1,0:T(8,128)(2,1)}), bf16[8,32,1792]{2,1,0:T(8,128)(2,1)S(1)}, u32[]{:S(2)}, u32[]{:S(2)}) %all-to-all-start.4) | async-done | bytes 917536 | tf_op jit(solution)/shard_map/all_to_all | solution.py:254
  121.1 8.9 %all-to-all-start.3 = ((bf16[8,32,1792]{2,1,0:T(8,128)(2,1)}), bf16[8,32,1792]{2,1,0:T(8,128)(2,1)S(1)}, u32[]{:S(2)}, u32[]{:S(2)}) async-start(bf16[8,32,1792]{2,1,0:T(8,128)(2,1)} %copy-done.1), calls=%async_computation.3 | async-start | bytes 1835008 | tf_op jit(solution)/shard_map/all_to_all | solution.py:254
  130.0 1.4 shard_map.97.rest_0_
  131.3 25.0 %all-to-all-done.3.back_ref = bf16[8,32,1792]{2,1,0:T(8,128)(2,1)S(1)} async-done(((bf16[8,32,1792]{2,1,0:T(8,128)(2,1)}), bf16[8,32,1792]{2,1,0:T(8,128)(2,1)S(1)}, u32[]{:S(2)}, u32[]{:S(2)}) %all-to-all-start.3) | async-done | bytes 917536 | tf_op jit(solution)/shard_map/all_to_all | solution.py:254
  156.4 1.4 shard_map.98
  (26 shorter events, 0.1 us)
Async XLA Ops:
  0.0 35.8 %copy-start = (f32[1,3584,4]{1,2,0:T(4,128)S(1)}, f32[1,3584,4]{1,2,0:T(4,128)}, u32[]{:S(2)}) copy-start(f32[1,3584,4]{1,2,0:T(4,128)} %param.17) | copy-start | bytes 172036
  0.0 4.4 %copy-start.9 = (bf16[2,1,1,32,16,128]{5,4,3,2,1,0:T(8,128)(2,1)S(1)}, bf16[2,1,1,32,16,128]{5,4,3,2,1,0:T(8,128)(2,1)}, u32[]{:S(2)}) copy-start(bf16[2,1,1,32,16,128]{5,4,3,2,1,0:T(8,128)(2,1)} %param.12) | copy-start | bytes 786436
  0.0 4.4 %copy-start.10 = (bf16[2,1,1,32,16,128]{5,4,3,2,1,0:T(8,128)(2,1)S(1)}, bf16[2,1,1,32,16,128]{5,4,3,2,1,0:T(8,128)(2,1)}, u32[]{:S(2)}) copy-start(bf16[2,1,1,32,16,128]{5,4,3,2,1,0:T(8,128)(2,1)} %param.13) | copy-start | bytes 786436
  1.3 13.7 %collective-permute-start = (bf16[64,3584]{1,0:T(8,128)(2,1)S(1)}, bf16[64,3584]{1,0:T(8,128)(2,1)S(1)}, u32[]{:S(2)}, u32[]{:S(2)}) collective-permute-start(bf16[64,3584]{1,0:T(8,128)(2,1)S(1)} %get-tuple-element.30), channel_id=1, source_target_pairs={{0,480},{32,0},{64,32},{96,64},{128,96},{160,128},{192,160},{224,1... | collective-permute-start | bytes 1376264 | tf_op jit(solution)/shard_map/ppermute | solution.py:21
  2.0 13.0 %collective-permute-start.1 = (bf16[64,3584]{1,0:T(8,128)(2,1)S(1)}, bf16[64,3584]{1,0:T(8,128)(2,1)S(1)}, u32[]{:S(2)}, u32[]{:S(2)}) collective-permute-start(bf16[64,3584]{1,0:T(8,128)(2,1)S(1)} %get-tuple-element.29), channel_id=1, source_target_pairs={{0,32},{32,64},{64,96},{96,128},{128,160},{160,192},{192,224},{224... | collective-permute-start | bytes 1376264 | tf_op jit(solution)/shard_map/ppermute | solution.py:21
  5.2 12.5 %all-to-all-start = ((bf16[4,2,2,128,128]{4,3,2,1,0:T(8,128)(2,1)}), bf16[4,2,2,128,128]{4,3,2,1,0:T(8,128)(2,1)S(1)}, u32[]{:S(2)}, u32[]{:S(2)}) async-start(bf16[4,2,2,128,128]{4,3,2,1,0:T(8,128)(2,1)} %shard_map.92), calls=%async_computation | async-start | bytes 1048576 | tf_op jit(solution)/shard_map/all_to_all | solution.py:254
  9.4 5.4 %copy-start.13 = (s32[2,1,64,1]{2,3,1,0:T(1,128)S(1)}, s32[2,1,64,1]{2,3,1,0:T(1,128)}, u32[]{:S(2)}) copy-start(s32[2,1,64,1]{2,3,1,0:T(1,128)} %param.10) | copy-start | bytes 1540
  9.4 5.5 %copy-start.14 = (bf16[2,1,64]{2,0,1:T(2,128)(2,1)S(1)}, bf16[2,1,64]{2,0,1:T(2,128)(2,1)}, u32[]{:S(2)}) copy-start(bf16[2,1,64]{2,0,1:T(2,128)(2,1)} %param.11) | copy-start | bytes 772
  9.4 26.6 %collective-permute-start.2 = (bf16[128,3584]{1,0:T(8,128)(2,1)}, bf16[128,3584]{1,0:T(8,128)(2,1)}, u32[]{:S(2)}, u32[]{:S(2)}) collective-permute-start(bf16[128,3584]{1,0:T(8,128)(2,1)} %bitcast.5.own_ref), channel_id=1, source_target_pairs={{0,1},{1,2},{2,3},{3,0},{4,5},{5,6},{6,7},{7,4},{8,9},{9,10},{10,1... | collective-permute-start | bytes 2752520 | tf_op jit(solution)/shard_map/ppermute | solution.py:27
  11.5 24.8 %collective-permute-start.3 = (bf16[128,3584]{1,0:T(8,128)(2,1)}, bf16[128,3584]{1,0:T(8,128)(2,1)}, u32[]{:S(2)}, u32[]{:S(2)}) collective-permute-start(bf16[128,3584]{1,0:T(8,128)(2,1)} %bitcast.5.own_ref), channel_id=1, source_target_pairs={{0,3},{1,0},{2,1},{3,2},{4,7},{5,4},{6,5},{7,6},{8,11},{9,8},{10,9... | collective-permute-start | bytes 2752520 | tf_op jit(solution)/shard_map/ppermute | solution.py:27
  16.8 0.9 copy-start.2
  17.8 37.2 %all-to-all-start.1 = ((bf16[8,16,3712]{2,1,0:T(8,128)(2,1)}), bf16[8,16,3712]{2,1,0:T(8,128)(2,1)S(1)}, u32[]{:S(2)}, u32[]{:S(2)}) async-start(bf16[8,16,3712]{2,1,0:T(8,128)(2,1)} %copy-done.2), calls=%async_computation.1 | async-start | bytes 1900544 | tf_op jit(solution)/shard_map/all_to_all | solution.py:254
  30.4 28.9 %collective-permute-start.6 = (bf16[2,1792,128]{2,1,0:T(8,128)(2,1)}, bf16[2,1792,128]{2,1,0:T(8,128)(2,1)}, u32[]{:S(2)}, u32[]{:S(2)}) collective-permute-start(bf16[2,1792,128]{2,1,0:T(8,128)(2,1)} %pad_maximum_fusion.1.own_ref), channel_id=1, source_target_pairs={{0,1},{1,2},{2,3},{3,0},{4,5},{5,6},{6,7},{7,4},{8,9},{9,10},{10,1... | collective-permute-start | bytes 2752520 | tf_op jit(solution)/shard_map/ppermute | solution.py:27
  33.7 30.1 %collective-permute-start.7 = (bf16[2,1792,128]{2,1,0:T(8,128)(2,1)}, bf16[2,1792,128]{2,1,0:T(8,128)(2,1)}, u32[]{:S(2)}, u32[]{:S(2)}) collective-permute-start(bf16[2,1792,128]{2,1,0:T(8,128)(2,1)} %pad_maximum_fusion.1.own_ref), channel_id=1, source_target_pairs={{0,3},{1,0},{2,1},{3,2},{4,7},{5,4},{6,5},{7,6},{8,11},{9,8},{10,9... | collective-permute-start | bytes 2752520 | tf_op jit(solution)/shard_map/ppermute | solution.py:27
  38.1 30.1 %collective-permute-start.4 = (bf16[64,3584]{1,0:T(8,128)(2,1)}, bf16[64,3584]{1,0:T(8,128)(2,1)}, u32[]{:S(2)}, u32[]{:S(2)}) collective-permute-start(bf16[64,3584]{1,0:T(8,128)(2,1)} %slice.56), channel_id=1, source_target_pairs={{0,1},{1,2},{2,3},{3,0},{4,5},{5,6},{6,7},{7,4},{8,9},{9,10},{10,1... | collective-permute-start | bytes 1376264 | tf_op jit(solution)/shard_map/ppermute | solution.py:27
  44.1 25.0 %collective-permute-start.5 = (bf16[64,3584]{1,0:T(8,128)(2,1)}, bf16[64,3584]{1,0:T(8,128)(2,1)}, u32[]{:S(2)}, u32[]{:S(2)}) collective-permute-start(bf16[64,3584]{1,0:T(8,128)(2,1)} %slice.57), channel_id=1, source_target_pairs={{0,3},{1,0},{2,1},{3,2},{4,7},{5,4},{6,5},{7,6},{8,11},{9,8},{10,9... | collective-permute-start | bytes 1376264 | tf_op jit(solution)/shard_map/ppermute | solution.py:27
  55.0 29.1 %all-to-all-start.2 = ((bf16[8,16,3712]{2,1,0:T(8,128)(2,1)}), bf16[8,16,3712]{2,1,0:T(8,128)(2,1)}, u32[]{:S(2)}, u32[]{:S(2)}) async-start(bf16[8,16,3712]{2,1,0:T(8,128)(2,1)} %get-tuple-element.21), calls=%async_computation.2 | async-start | bytes 1900544 | tf_op jit(solution)/shard_map/all_to_all | solution.py:254
  61.1 26.6 %collective-permute-start.12 = (bf16[1792,128]{1,0:T(8,128)(2,1)}, bf16[1792,128]{1,0:T(8,128)(2,1)}, u32[]{:S(2)}, u32[]{:S(2)}) collective-permute-start(bf16[1792,128]{1,0:T(8,128)(2,1)} %slice_bitcast_fusion.1), channel_id=1, source_target_pairs={{0,1},{1,2},{2,3},{3,0},{4,5},{5,6},{6,7},{7,4},{8,9},{9,10},{10,1... | collective-permute-start | bytes 1376264 | tf_op jit(solution)/shard_map/ppermute | solution.py:27
  65.7 22.0 %collective-permute-start.13 = (bf16[1792,128]{1,0:T(8,128)(2,1)}, bf16[1792,128]{1,0:T(8,128)(2,1)}, u32[]{:S(2)}, u32[]{:S(2)}) collective-permute-start(bf16[1792,128]{1,0:T(8,128)(2,1)} %slice_bitcast_fusion), channel_id=1, source_target_pairs={{0,3},{1,0},{2,1},{3,2},{4,7},{5,4},{6,5},{7,6},{8,11},{9,8},{10,9... | collective-permute-start | bytes 1376264 | tf_op jit(solution)/shard_map/ppermute | solution.py:27
  69.1 27.7 %collective-permute-start.8 = (bf16[2,1792,128]{2,1,0:T(8,128)(2,1)S(1)}, bf16[2,1792,128]{2,1,0:T(8,128)(2,1)}, u32[]{:S(2)}, u32[]{:S(2)}) collective-permute-start(bf16[2,1792,128]{2,1,0:T(8,128)(2,1)S(1)} %pad_maximum_fusion.own_ref), channel_id=1, source_target_pairs={{0,1},{1,2},{2,3},{3,0},{4,5},{5,6},{6,7},{7,4},{8,9},{9,10},{10,1... | collective-permute-start | bytes 2752520 | tf_op jit(solution)/shard_map/ppermute | solution.py:27
  72.2 29.0 %collective-permute-start.9 = (bf16[2,1792,128]{2,1,0:T(8,128)(2,1)S(1)}, bf16[2,1792,128]{2,1,0:T(8,128)(2,1)}, u32[]{:S(2)}, u32[]{:S(2)}) collective-permute-start(bf16[2,1792,128]{2,1,0:T(8,128)(2,1)S(1)} %pad_maximum_fusion.own_ref), channel_id=1, source_target_pairs={{0,3},{1,0},{2,1},{3,2},{4,7},{5,4},{6,5},{7,6},{8,11},{9,8},{10,9... | collective-permute-start | bytes 2752520 | tf_op jit(solution)/shard_map/ppermute | solution.py:27
  77.6 0.7 copy-start.4
  84.1 3.6 %copy-start.5 = (bf16[128,1024]{1,0:T(8,128)(2,1)S(1)}, bf16[128,1024]{1,0:T(8,128)(2,1)}, u32[]{:S(2)}) copy-start(bf16[128,1024]{1,0:T(8,128)(2,1)} %copy-done.4) | copy-start | bytes 786436
  91.0 0.9 copy-start.3
  91.9 0.7 copy-start.7
  92.6 0.6 copy-start.11
  93.3 27.8 %all-to-all-start.4 = ((bf16[8,32,1792]{2,1,0:T(8,128)(2,1)}), bf16[8,32,1792]{2,1,0:T(8,128)(2,1)S(1)}, u32[]{:S(2)}, u32[]{:S(2)}) async-start(bf16[8,32,1792]{2,1,0:T(8,128)(2,1)} %copy-done.3), calls=%async_computation.4 | async-start | bytes 1835008 | tf_op jit(solution)/shard_map/all_to_all | solution.py:254
  97.9 17.0 %copy-start.6 = (bf16[128,1024]{1,0:T(8,128)(2,1)S(1)}, bf16[128,1024]{1,0:T(8,128)(2,1)}, u32[]{:S(2)}) copy-start(bf16[128,1024]{1,0:T(8,128)(2,1)} %copy-done.4) | copy-start | bytes 786436
  97.9 17.0 %copy-start.8 = (bf16[128,1024]{1,0:T(8,128)(2,1)S(1)}, bf16[128,1024]{1,0:T(8,128)(2,1)}, u32[]{:S(2)}) copy-start(bf16[128,1024]{1,0:T(8,128)(2,1)} %copy-done.7) | copy-start | bytes 786436
  97.9 17.0 %copy-start.12 = (f32[128,128]{1,0:T(8,128)S(1)}, f32[128,128]{1,0:T(8,128)}, u32[]{:S(2)}) copy-start(f32[128,128]{1,0:T(8,128)} %copy-done.11) | copy-start | bytes 196612
  97.9 11.3 %collective-permute-start.10 = (bf16[1792,128]{1,0:T(8,128)(2,1)S(1)}, bf16[1792,128]{1,0:T(8,128)(2,1)S(1)}, u32[]{:S(2)}, u32[]{:S(2)}) collective-permute-start(bf16[1792,128]{1,0:T(8,128)(2,1)S(1)} %slice_bitcast_fusion.3), channel_id=1, source_target_pairs={{0,1},{1,2},{2,3},{3,0},{4,5},{5,6},{6,7},{7,4},{8,9},{9,10},{10,1... | collective-permute-start | bytes 1376264 | tf_op jit(solution)/shard_map/ppermute | solution.py:27
  102.3 12.6 %collective-permute-start.11 = (bf16[1792,128]{1,0:T(8,128)(2,1)S(1)}, bf16[1792,128]{1,0:T(8,128)(2,1)S(1)}, u32[]{:S(2)}, u32[]{:S(2)}) collective-permute-start(bf16[1792,128]{1,0:T(8,128)(2,1)S(1)} %slice_bitcast_fusion.2), channel_id=1, source_target_pairs={{0,3},{1,0},{2,1},{3,2},{4,7},{5,4},{6,5},{7,6},{8,11},{9,8},{10,9... | collective-permute-start | bytes 1376264 | tf_op jit(solution)/shard_map/ppermute | solution.py:27
  117.6 0.9 copy-start.1
  121.1 35.3 %all-to-all-start.3 = ((bf16[8,32,1792]{2,1,0:T(8,128)(2,1)}), bf16[8,32,1792]{2,1,0:T(8,128)(2,1)S(1)}, u32[]{:S(2)}, u32[]{:S(2)}) async-start(bf16[8,32,1792]{2,1,0:T(8,128)(2,1)} %copy-done.1), calls=%async_computation.3 | async-start | bytes 1835008 | tf_op jit(solution)/shard_map/all_to_all | solution.py:254

commit v3 on v2

--- a/solution.py
+++ b/solution.py
@@ -11,6 +11,7 @@
 F32 = jnp.float32
 LANE = 128
 FLOPS = (10000000000, 1000000000)
+NEAR = 10**9
 RING = 4
 VMEM_LIMIT = 48 * 1024 * 1024
 
@@ -204,6 +205,71 @@
     )(first, first_scaled, second, second_scaled, router, *weights)
 
 
+def near_kernel(
+    first_ref,
+    first_scaled_ref,
+    second_ref,
+    second_scaled_ref,
+    router_ref,
+    own_ref,
+    left_ref,
+    right_ref,
+    out_ref,
+):
+    units = own_ref.shape[2]
+    depth = 2 * units
+    grads = jnp.concatenate([first_ref[...], second_ref[...]], axis=0)
+    grads = jnp.concatenate([grads[:, : 2 * depth], grads[:, 3 * depth :]], axis=1)
+    scaled = jnp.concatenate([first_scaled_ref[...], second_scaled_ref[...]], axis=0)[:, :1]
+    block = out_ref.shape[1] // 2
+    for part in range(2):
+        span = slice(part * block, (part + 1) * block)
+        weights = [ref[which, span] for ref in (own_ref, right_ref, left_ref) for which in range(2)]
+        weights = jnp.concatenate(weights, axis=1)
+        out_ref[:, span] = dot(grads, weights, ((1,), (1,))) + scaled * router_ref[:, span]
+
+
+def far_kernel(first_ref, second_ref, near_ref, gate_ref, up_ref, out_ref):
+    planes, two, width = out_ref.shape
+    capacity = two // 2
+    count = planes * capacity
+    depth = 2 * gate_ref.shape[1]
+    columns = slice(2 * depth, 3 * depth)
+    grads = jnp.concatenate([first_ref[:, columns], second_ref[:, columns]], axis=0)
+    block = width // 2
+    for part in range(2):
+        span = slice(part * block, (part + 1) * block)
+        weights = jnp.concatenate([gate_ref[span], up_ref[span]], axis=1)
+        total = (near_ref[:, span] + dot(grads, weights, ((1,), (1,)))).astype(BF)
+        for way in range(2):
+            piece = total[way * count : (way + 1) * count].reshape(planes, capacity, block)
+            out_ref[:, way * capacity : (way + 1) * capacity, span] = piece
+
+
+def late_parts(flops, grads, router, weights, capacity):
+    (first, first_scaled), (second, second_scaled) = grads
+    own, left, right, gate, up = weights
+    width = router.shape[1]
+    count = first.shape[0]
+    whole = pl.BlockSpec(memory_space=pltpu.VMEM)
+    params = pltpu.CompilerParams(vmem_limit_bytes=VMEM_LIMIT)
+    near = pl.pallas_call(
+        near_kernel,
+        in_specs=[whole] * 8,
+        out_specs=whole,
+        out_shape=jax.ShapeDtypeStruct((2 * count, width), F32),
+        compiler_params=params,
+        cost_estimate=pl.CostEstimate(flops=NEAR, bytes_accessed=5 * 10**6, transcendentals=0),
+    )(first, first_scaled, second, second_scaled, router, own, left, right)
+    return pl.pallas_call(
+        far_kernel,
+        in_specs=[whole] * 5,
+        out_shape=jax.ShapeDtypeStruct((count // capacity, 2 * capacity, width), BF),
+        compiler_params=params,
+        cost_estimate=pl.CostEstimate(flops=flops, bytes_accessed=5 * 10**6, transcendentals=0),
+    )(first, second, near, gate, up)
+
+
 def finish_kernel(experts, capacity, routes_ref, first_ref, second_ref, back_ref, *rest):
     out_ref = rest[-1]
     planes, _, width = back_ref.shape
@@ -287,7 +353,8 @@
     grads = [hidden_grads(way, place, toks[way], saved, down) for way in range(2)]
     out = None
     for part in range(2):
-        parts = input_parts(FLOPS[part], grads, router[:, spans[part]], weights[part], capacity)
+        compute = input_parts if part == 0 else late_parts
+        parts = compute(FLOPS[part], grads, router[:, spans[part]], weights[part], capacity)
         back = exchange(parts, along_z)
         out = finish(part, routes, incoming, back, experts, capacity, out)
     return out[:, None]

time: 159 us -> 157 us (0.987)
  the two profiles are of different devices: /device:TPU:31 before, /device:TPU:24 now
where the time goes in v3:
time: 157 us; the launch traced here: 155 us
  starting transfers between devices  68.7 us (44%)
  waiting for transfers between devices  49.6 us (32%)
  Pallas kernels  18.3 us (12%)
  local copies, waits for them, and re-layouts  17.3 us (11%)
    all_to_all x5, waiting for transfers between devices, exchange(): lax.all_to_all(value, 'expert', split_axis=0, concat_axis=0, axis_index_g...  43.6 us
    ppermute x12, starting transfers between devices, turned(): return lax.ppermute(value, 'expert', pairs)  42.3 us
    all_to_all x5, starting transfers between devices, exchange(): lax.all_to_all(value, 'expert', split_axis=0, concat_axis=0, axis_index_g...  25.9 us
    pallas_call x2, Pallas kernels, hidden_grads(): pl.pallas_call(functools.partial(hidden_kernel, way), in_specs=[pl.BlockS...  6.71 us
    ppermute x12, waiting for transfers between devices, turned(): return lax.ppermute(value, 'expert', pairs)  6.03 us
    unnamed x24, local copies, waits for them, and re-layouts  4.99 us
    squeeze x2, local copies, waits for them, and re-layouts, per_device(): af, ag = (turned(al[0], 1), turned(ar[1], RING - 1))  3.67 us
    slice x2, local copies, waits for them, and re-layouts, per_device(): wf, wg = (turned(wl[:half], 1), turned(wr[half:], RING - 1))  3.66 us
  transfers between devices with their start and end apart: 19, of which 6 were waited for; matrix products, arithmetic and copies ran while one was open for 8% of the time, Pallas kernels for 11%

profile of v3, /device:TPU:24, one launch (start us, length us, event | category | flops | bytes accessed | tf_op | source)
XLA Modules:
  0.0 155.4 jit_solution(14600369461542554816)
XLA Ops:
  0.0 1.3 slice_bitcast_fusion.4
  1.3 0.0 collective-permute-start
  1.3 0.5 collective-permute-start.1
  1.8 0.8 shard_map.92
  2.7 4.3 %all-to-all-start = ((bf16[4,2,2,128,128]{4,3,2,1,0:T(8,128)(2,1)}), bf16[4,2,2,128,128]{4,3,2,1,0:T(8,128)(2,1)S(1)}, u32[]{:S(2)}, u32[]{:S(2)}) async-start(bf16[4,2,2,128,128]{4,3,2,1,0:T(8,128)(2,1)} %shard_map.92), calls=%async_computation | async-start | bytes 1048576 | tf_op jit(solution)/shard_map/all_to_all | solution.py:320
  7.0 3.9 %collective-permute-start.2 = (bf16[128,3584]{1,0:T(8,128)(2,1)}, bf16[128,3584]{1,0:T(8,128)(2,1)}, u32[]{:S(2)}, u32[]{:S(2)}) collective-permute-start(bf16[128,3584]{1,0:T(8,128)(2,1)} %bitcast.5.own_ref), channel_id=1, source_target_pairs={{0,1},{1,2},{2,3},{3,0},{4,5},{5,6},{6,7},{7,4},{8,9},{9,10},{10,1... | collective-permute-start | bytes 2752520 | tf_op jit(solution)/shard_map/ppermute | solution.py:28
  10.9 3.1 %collective-permute-start.3 = (bf16[128,3584]{1,0:T(8,128)(2,1)}, bf16[128,3584]{1,0:T(8,128)(2,1)}, u32[]{:S(2)}, u32[]{:S(2)}) collective-permute-start(bf16[128,3584]{1,0:T(8,128)(2,1)} %bitcast.5.own_ref), channel_id=1, source_target_pairs={{0,3},{1,0},{2,1},{3,2},{4,7},{5,4},{6,5},{7,6},{8,11},{9,8},{10,9... | collective-permute-start | bytes 2752520 | tf_op jit(solution)/shard_map/ppermute | solution.py:28
  14.0 0.1 copy.14.routes_ref
  14.2 0.0 collective-permute-done.rest_0_.first_ref
  14.2 0.0 collective-permute-done.1.rest_1_.second_ref
  14.2 1.8 %shard_map.91 = (bf16[8,16,3712]{2,1,0:T(8,128)(2,1)S(1)}, bf16[8,16,3712]{2,1,0:T(8,128)(2,1)}) custom-call(s32[2,1,64,1]{3,2,1,0:T(8,128)S(1)} %copy.14.routes_ref, bf16[2,1,64]{2,1,0:T(2,128)(2,1)S(1)} %copy.12.probs_ref, bf16[64,3584]{1,0:T(8,128)(2,1)S(1)} %collective-permute-done.rest_0_.first_ref, ...), custom_call_target="tpu_custom_call" | custom-call | flops 100000000 | bytes 4000000 | tf_op jit(solution)/shard_map/pallas_call | solution.py:81
  16.0 0.9 copy-done.2
  16.9 0.0 all-to-all-done.saved_ref
  16.9 10.3 %all-to-all-start.1 = ((bf16[8,16,3712]{2,1,0:T(8,128)(2,1)}), bf16[8,16,3712]{2,1,0:T(8,128)(2,1)S(1)}, u32[]{:S(2)}, u32[]{:S(2)}) async-start(bf16[8,16,3712]{2,1,0:T(8,128)(2,1)} %copy-done.2), calls=%async_computation.1 | async-start | bytes 1900544 | tf_op jit(solution)/shard_map/all_to_all | solution.py:320
  27.3 1.6 fusion
  28.8 1.0 pad_maximum_fusion.1.own_ref
  29.8 2.7 %collective-permute-start.6 = (bf16[2,1792,128]{2,1,0:T(8,128)(2,1)}, bf16[2,1792,128]{2,1,0:T(8,128)(2,1)}, u32[]{:S(2)}, u32[]{:S(2)}) collective-permute-start(bf16[2,1792,128]{2,1,0:T(8,128)(2,1)} %pad_maximum_fusion.1.own_ref), channel_id=1, source_target_pairs={{0,1},{1,2},{2,3},{3,0},{4,5},{5,6},{6,7},{7,4},{8,9},{9,10},{10,1... | collective-permute-start | bytes 2752520 | tf_op jit(solution)/shard_map/ppermute | solution.py:28
  32.6 4.3 %collective-permute-start.7 = (bf16[2,1792,128]{2,1,0:T(8,128)(2,1)}, bf16[2,1792,128]{2,1,0:T(8,128)(2,1)}, u32[]{:S(2)}, u32[]{:S(2)}) collective-permute-start(bf16[2,1792,128]{2,1,0:T(8,128)(2,1)} %pad_maximum_fusion.1.own_ref), channel_id=1, source_target_pairs={{0,3},{1,0},{2,1},{3,2},{4,7},{5,4},{6,5},{7,6},{8,11},{9,8},{10,9... | collective-permute-start | bytes 2752520 | tf_op jit(solution)/shard_map/ppermute | solution.py:28
  36.9 0.1 pad_maximum_fusion.own_ref
  37.1 0.0 collective-permute-done.2.left_ref
  37.1 0.0 collective-permute-done.3.right_ref
  37.1 1.8 %slice.56 = bf16[64,3584]{1,0:T(8,128)(2,1)} slice(bf16[128,3584]{1,0:T(8,128)(2,1)} %collective-permute-done.2.left_ref), slice={[0:64], [0:3584]} | slice | bytes 917504 | tf_op jit(solution)/shard_map/slice | solution.py:333
  38.9 2.8 %collective-permute-start.4 = (bf16[64,3584]{1,0:T(8,128)(2,1)}, bf16[64,3584]{1,0:T(8,128)(2,1)}, u32[]{:S(2)}, u32[]{:S(2)}) collective-permute-start(bf16[64,3584]{1,0:T(8,128)(2,1)} %slice.56), channel_id=1, source_target_pairs={{0,1},{1,2},{2,3},{3,0},{4,5},{5,6},{6,7},{7,4},{8,9},{9,10},{10,1... | collective-permute-start | bytes 1376264 | tf_op jit(solution)/shard_map/ppermute | solution.py:28
  41.7 1.8 %slice.57 = bf16[64,3584]{1,0:T(8,128)(2,1)} slice(bf16[128,3584]{1,0:T(8,128)(2,1)} %collective-permute-done.3.right_ref), slice={[64:128], [0:3584]} | slice | bytes 917504 | tf_op jit(solution)/shard_map/slice | solution.py:333
  43.5 4.2 %collective-permute-start.5 = (bf16[64,3584]{1,0:T(8,128)(2,1)}, bf16[64,3584]{1,0:T(8,128)(2,1)}, u32[]{:S(2)}, u32[]{:S(2)}) collective-permute-start(bf16[64,3584]{1,0:T(8,128)(2,1)} %slice.57), channel_id=1, source_target_pairs={{0,3},{1,0},{2,1},{3,2},{4,7},{5,4},{6,5},{7,6},{8,11},{9,8},{10,9... | collective-permute-start | bytes 1376264 | tf_op jit(solution)/shard_map/ppermute | solution.py:28
  47.8 7.4 %all-to-all-done.1.tok_ref = bf16[8,16,3712]{2,1,0:T(8,128)(2,1)S(1)} async-done(((bf16[8,16,3712]{2,1,0:T(8,128)(2,1)}), bf16[8,16,3712]{2,1,0:T(8,128)(2,1)S(1)}, u32[]{:S(2)}, u32[]{:S(2)}) %all-to-all-start.1) | async-done | bytes 950304 | tf_op jit(solution)/shard_map/all_to_all | solution.py:320
  55.2 4.2 %all-to-all-start.2 = ((bf16[8,16,3712]{2,1,0:T(8,128)(2,1)}), bf16[8,16,3712]{2,1,0:T(8,128)(2,1)}, u32[]{:S(2)}, u32[]{:S(2)}) async-start(bf16[8,16,3712]{2,1,0:T(8,128)(2,1)} %get-tuple-element.20), calls=%async_computation.2 | async-start | bytes 1900544 | tf_op jit(solution)/shard_map/all_to_all | solution.py:320
  59.5 0.0 collective-permute-done.6.left_ref
  59.5 1.8 %slice_bitcast_fusion.1 = bf16[1792,128]{1,0:T(8,128)(2,1)} fusion(bf16[2,1792,128]{2,1,0:T(8,128)(2,1)} %collective-permute-done.6.left_ref), kind=kLoop, calls=%fused_computation.3 | loop fusion | bytes 917504 | tf_op jit(solution)/shard_map/squeeze | solution.py:338
  61.3 2.9 %collective-permute-start.12 = (bf16[1792,128]{1,0:T(8,128)(2,1)}, bf16[1792,128]{1,0:T(8,128)(2,1)}, u32[]{:S(2)}, u32[]{:S(2)}) collective-permute-start(bf16[1792,128]{1,0:T(8,128)(2,1)} %slice_bitcast_fusion.1), channel_id=1, source_target_pairs={{0,1},{1,2},{2,3},{3,0},{4,5},{5,6},{6,7},{7,4},{8,9},{9,10},{10,1... | collective-permute-start | bytes 1376264 | tf_op jit(solution)/shard_map/ppermute | solution.py:28
  64.2 0.0 collective-permute-done.7.right_ref
  64.2 1.8 %slice_bitcast_fusion = bf16[1792,128]{1,0:T(8,128)(2,1)} fusion(bf16[2,1792,128]{2,1,0:T(8,128)(2,1)} %collective-permute-done.7.right_ref), kind=kLoop, calls=%fused_computation.2 | loop fusion | bytes 917504 | tf_op jit(solution)/shard_map/squeeze | solution.py:338
  66.0 4.2 %collective-permute-start.13 = (bf16[1792,128]{1,0:T(8,128)(2,1)}, bf16[1792,128]{1,0:T(8,128)(2,1)}, u32[]{:S(2)}, u32[]{:S(2)}) collective-permute-start(bf16[1792,128]{1,0:T(8,128)(2,1)} %slice_bitcast_fusion), channel_id=1, source_target_pairs={{0,3},{1,0},{2,1},{3,2},{4,7},{5,4},{6,5},{7,6},{8,11},{9,8},{10,9... | collective-permute-start | bytes 1376264 | tf_op jit(solution)/shard_map/ppermute | solution.py:28
  70.2 0.0 collective-permute-done.4.low_ref
  70.2 0.0 collective-permute-done.5.high_ref
  70.2 1.9 %collective-permute-start.8 = (bf16[2,1792,128]{2,1,0:T(8,128)(2,1)S(1)}, bf16[2,1792,128]{2,1,0:T(8,128)(2,1)}, u32[]{:S(2)}, u32[]{:S(2)}) collective-permute-start(bf16[2,1792,128]{2,1,0:T(8,128)(2,1)S(1)} %pad_maximum_fusion.own_ref), channel_id=1, source_target_pairs={{0,1},{1,2},{2,3},{3,0},{4,5},{5,6},{6,7},{7,4},{8,9},{9,10},{10,1... | collective-permute-start | bytes 2752520 | tf_op jit(solution)/shard_map/ppermute | solution.py:28
  72.2 5.1 %collective-permute-start.9 = (bf16[2,1792,128]{2,1,0:T(8,128)(2,1)S(1)}, bf16[2,1792,128]{2,1,0:T(8,128)(2,1)}, u32[]{:S(2)}, u32[]{:S(2)}) collective-permute-start(bf16[2,1792,128]{2,1,0:T(8,128)(2,1)S(1)} %pad_maximum_fusion.own_ref), channel_id=1, source_target_pairs={{0,3},{1,0},{2,1},{3,2},{4,7},{5,4},{6,5},{7,6},{8,11},{9,8},{10,9... | collective-permute-start | bytes 2752520 | tf_op jit(solution)/shard_map/ppermute | solution.py:28
  77.3 1.0 copy-done.5
  78.3 3.2 %shard_map.93 = (bf16[128,1024]{1,0:T(8,128)(2,1)S(1)}, f32[128,128]{1,0:T(8,128)S(1)}) custom-call(s32[1]{0:T(128)} %bitcast.2.place_ref, bf16[8,16,3712]{2,1,0:T(8,128)(2,1)S(1)} %all-to-all-done.1.tok_ref, bf16[4,2,2,128,128]{4,3,2,1,0:T(8,128)(2,1)S(1)} %copy-done.5, bf16[128,3584]{1,0:T(8,128)(2,1)} %bitcast.5.own_ref, ...), custom_call_target="tpu_custom_call" | custom-call | flops 10000000000 | bytes 5000000 | tf_op jit(solution)/shard_map/pallas_call | solution.py:141
  81.6 5.1 %all-to-all-done.2.tok_ref = bf16[8,16,3712]{2,1,0:T(8,128)(2,1)} async-done(((bf16[8,16,3712]{2,1,0:T(8,128)(2,1)}), bf16[8,16,3712]{2,1,0:T(8,128)(2,1)}, u32[]{:S(2)}, u32[]{:S(2)}) %all-to-all-start.2) | async-done | bytes 950304 | tf_op jit(solution)/shard_map/all_to_all | solution.py:320
  86.7 1.0 copy-done.6
  87.7 3.5 %shard_map.94 = (bf16[128,1024]{1,0:T(8,128)(2,1)S(1)}, f32[128,128]{1,0:T(8,128)S(1)}) custom-call(s32[1]{0:T(128)} %bitcast.2.place_ref, bf16[8,16,3712]{2,1,0:T(8,128)(2,1)} %all-to-all-done.2.tok_ref, bf16[4,2,2,128,128]{4,3,2,1,0:T(8,128)(2,1)S(1)} %copy-done.6, bf16[128,3584]{1,0:T(8,128)(2,1)} %bitcast.5.own_ref, ...), custom_call_target="tpu_custom_call" | custom-call | flops 10000000000 | bytes 5000000 | tf_op jit(solution)/shard_map/pallas_call | solution.py:141
  91.2 0.0 collective-permute-done.12.gate_ref
  91.2 0.0 collective-permute-done.13.up_ref
  91.2 3.3 %shard_map.97 = bf16[8,32,1792]{2,1,0:T(8,128)(2,1)S(1)} custom-call(bf16[128,1024]{1,0:T(8,128)(2,1)S(1)} %get-tuple-element.18.first_ref, f32[128,128]{1,0:T(8,128)S(1)} %get-tuple-element.22.first_scaled_ref, bf16[128,1024]{1,0:T(8,128)(2,1)S(1)} %get-tuple-element.21.second_ref, f32[128,128]{1,0:T(8,128)S(1)} %get-tuple-element.23.second_scaled_ref, ...), custom_call_target="tpu_custom_call" | custom-call | flops 10000000000 | bytes 5000000 | tf_op jit(solution)/shard_map/pallas_call | solution.py:199
  94.5 0.0 copy-start.3
  94.5 0.9 copy-done.3
  95.4 3.6 %all-to-all-start.4 = ((bf16[8,32,1792]{2,1,0:T(8,128)(2,1)}), bf16[8,32,1792]{2,1,0:T(8,128)(2,1)S(1)}, u32[]{:S(2)}, u32[]{:S(2)}) async-start(bf16[8,32,1792]{2,1,0:T(8,128)(2,1)} %copy-done.3), calls=%async_computation.4 | async-start | bytes 1835008 | tf_op jit(solution)/shard_map/all_to_all | solution.py:320
  99.0 0.0 collective-permute-done.8.left_ref
  99.0 1.0 slice_bitcast_fusion.3
  100.0 2.8 %collective-permute-start.10 = (bf16[1792,128]{1,0:T(8,128)(2,1)S(1)}, bf16[1792,128]{1,0:T(8,128)(2,1)S(1)}, u32[]{:S(2)}, u32[]{:S(2)}) collective-permute-start(bf16[1792,128]{1,0:T(8,128)(2,1)S(1)} %slice_bitcast_fusion.3), channel_id=1, source_target_pairs={{0,1},{1,2},{2,3},{3,0},{4,5},{5,6},{6,7},{7,4},{8,9},{9,10},{10,1... | collective-permute-start | bytes 1376264 | tf_op jit(solution)/shard_map/ppermute | solution.py:28
  102.9 0.0 collective-permute-done.9.right_ref
  102.9 1.1 slice_bitcast_fusion.2
  103.9 4.2 %collective-permute-start.11 = (bf16[1792,128]{1,0:T(8,128)(2,1)S(1)}, bf16[1792,128]{1,0:T(8,128)(2,1)S(1)}, u32[]{:S(2)}, u32[]{:S(2)}) collective-permute-start(bf16[1792,128]{1,0:T(8,128)(2,1)S(1)} %slice_bitcast_fusion.2), channel_id=1, source_target_pairs={{0,3},{1,0},{2,1},{3,2},{4,7},{5,4},{6,5},{7,6},{8,11},{9,8},{10,9... | collective-permute-start | bytes 1376264 | tf_op jit(solution)/shard_map/ppermute | solution.py:28
  108.2 2.5 %shard_map.95.near_ref = f32[256,1792]{1,0:T(8,128)S(1)} custom-call(bf16[128,1024]{1,0:T(8,128)(2,1)S(1)} %get-tuple-element.18.first_ref, f32[128,128]{1,0:T(8,128)S(1)} %get-tuple-element.22.first_scaled_ref, bf16[128,1024]{1,0:T(8,128)(2,1)S(1)} %get-tuple-element.21.second_ref, f32[128,128]{1,0:T(8,128)S(1)} %get-tuple-element.23.second_scaled_ref, ...), custom_call_target="tpu_custom_call" | custom-call | flops 1000000000 | bytes 5000000 | tf_op jit(solution)/shard_map/pallas_call | solution.py:256
  110.7 3.8 %collective-permute-done.10.gate_ref = bf16[1792,128]{1,0:T(8,128)(2,1)S(1)} collective-permute-done((bf16[1792,128]{1,0:T(8,128)(2,1)S(1)}, bf16[1792,128]{1,0:T(8,128)(2,1)S(1)}, u32[]{:S(2)}, u32[]{:S(2)}) %collective-permute-start.10) | collective-permute-done | bytes 458784 | tf_op jit(solution)/shard_map/ppermute | solution.py:28
  114.4 2.2 %collective-permute-done.11.up_ref = bf16[1792,128]{1,0:T(8,128)(2,1)S(1)} collective-permute-done((bf16[1792,128]{1,0:T(8,128)(2,1)S(1)}, bf16[1792,128]{1,0:T(8,128)(2,1)S(1)}, u32[]{:S(2)}, u32[]{:S(2)}) %collective-permute-start.11) | collective-permute-done | bytes 458784 | tf_op jit(solution)/shard_map/ppermute | solution.py:28
  116.7 0.5 shard_map.96
  117.1 0.9 copy-done.1
  118.1 6.1 %all-to-all-done.4.back_ref = bf16[8,32,1792]{2,1,0:T(8,128)(2,1)S(1)} async-done(((bf16[8,32,1792]{2,1,0:T(8,128)(2,1)}), bf16[8,32,1792]{2,1,0:T(8,128)(2,1)S(1)}, u32[]{:S(2)}, u32[]{:S(2)}) %all-to-all-start.4) | async-done | bytes 917536 | tf_op jit(solution)/shard_map/all_to_all | solution.py:320
  124.2 3.6 %all-to-all-start.3 = ((bf16[8,32,1792]{2,1,0:T(8,128)(2,1)}), bf16[8,32,1792]{2,1,0:T(8,128)(2,1)S(1)}, u32[]{:S(2)}, u32[]{:S(2)}) async-start(bf16[8,32,1792]{2,1,0:T(8,128)(2,1)} %copy-done.1), calls=%async_computation.3 | async-start | bytes 1835008 | tf_op jit(solution)/shard_map/all_to_all | solution.py:320
  127.7 1.4 shard_map.98.rest_0_
  129.1 24.9 %all-to-all-done.3.back_ref = bf16[8,32,1792]{2,1,0:T(8,128)(2,1)S(1)} async-done(((bf16[8,32,1792]{2,1,0:T(8,128)(2,1)}), bf16[8,32,1792]{2,1,0:T(8,128)(2,1)S(1)}, u32[]{:S(2)}, u32[]{:S(2)}) %all-to-all-start.3) | async-done | bytes 917536 | tf_op jit(solution)/shard_map/all_to_all | solution.py:320
  154.0 1.4 shard_map.99
  (19 shorter events, 0.1 us)
Async XLA Ops:
  0.0 37.0 %copy-start = (f32[1,3584,4]{1,2,0:T(4,128)S(1)}, f32[1,3584,4]{1,2,0:T(4,128)}, u32[]{:S(2)}) copy-start(f32[1,3584,4]{1,2,0:T(4,128)} %param.17) | copy-start | bytes 172036
  0.0 1.8 %copy-start.7 = (bf16[2,1,1,32,16,128]{5,4,3,2,1,0:T(8,128)(2,1)S(1)}, bf16[2,1,1,32,16,128]{5,4,3,2,1,0:T(8,128)(2,1)}, u32[]{:S(2)}) copy-start(bf16[2,1,1,32,16,128]{5,4,3,2,1,0:T(8,128)(2,1)} %param.12) | copy-start | bytes 786436
  0.0 1.8 %copy-start.8 = (bf16[2,1,1,32,16,128]{5,4,3,2,1,0:T(8,128)(2,1)S(1)}, bf16[2,1,1,32,16,128]{5,4,3,2,1,0:T(8,128)(2,1)}, u32[]{:S(2)}) copy-start(bf16[2,1,1,32,16,128]{5,4,3,2,1,0:T(8,128)(2,1)} %param.13) | copy-start | bytes 786436
  0.0 14.0 %copy-start.9 = (s32[2,1,64,1]{2,3,1,0:T(1,128)S(1)}, s32[2,1,64,1]{2,3,1,0:T(1,128)}, u32[]{:S(2)}) copy-start(s32[2,1,64,1]{2,3,1,0:T(1,128)} %param.10) | copy-start | bytes 1540
  0.0 14.1 %copy-start.10 = (bf16[2,1,64]{2,0,1:T(2,128)(2,1)S(1)}, bf16[2,1,64]{2,0,1:T(2,128)(2,1)}, u32[]{:S(2)}) copy-start(bf16[2,1,64]{2,0,1:T(2,128)(2,1)} %param.11) | copy-start | bytes 772
  1.3 12.9 %collective-permute-start = (bf16[64,3584]{1,0:T(8,128)(2,1)S(1)}, bf16[64,3584]{1,0:T(8,128)(2,1)S(1)}, u32[]{:S(2)}, u32[]{:S(2)}) collective-permute-start(bf16[64,3584]{1,0:T(8,128)(2,1)S(1)} %get-tuple-element.30), channel_id=1, source_target_pairs={{0,480},{32,0},{64,32},{96,64},{128,96},{160,128},{192,160},{224,1... | collective-permute-start | bytes 1376264 | tf_op jit(solution)/shard_map/ppermute | solution.py:22
  1.3 12.9 %collective-permute-start.1 = (bf16[64,3584]{1,0:T(8,128)(2,1)S(1)}, bf16[64,3584]{1,0:T(8,128)(2,1)S(1)}, u32[]{:S(2)}, u32[]{:S(2)}) collective-permute-start(bf16[64,3584]{1,0:T(8,128)(2,1)S(1)} %get-tuple-element.29), channel_id=1, source_target_pairs={{0,32},{32,64},{64,96},{96,128},{128,160},{160,192},{192,224},{224... | collective-permute-start | bytes 1376264 | tf_op jit(solution)/shard_map/ppermute | solution.py:22
  2.7 14.3 %all-to-all-start = ((bf16[4,2,2,128,128]{4,3,2,1,0:T(8,128)(2,1)}), bf16[4,2,2,128,128]{4,3,2,1,0:T(8,128)(2,1)S(1)}, u32[]{:S(2)}, u32[]{:S(2)}) async-start(bf16[4,2,2,128,128]{4,3,2,1,0:T(8,128)(2,1)} %shard_map.92), calls=%async_computation | async-start | bytes 1048576 | tf_op jit(solution)/shard_map/all_to_all | solution.py:320
  7.0 30.1 %collective-permute-start.2 = (bf16[128,3584]{1,0:T(8,128)(2,1)}, bf16[128,3584]{1,0:T(8,128)(2,1)}, u32[]{:S(2)}, u32[]{:S(2)}) collective-permute-start(bf16[128,3584]{1,0:T(8,128)(2,1)} %bitcast.5.own_ref), channel_id=1, source_target_pairs={{0,1},{1,2},{2,3},{3,0},{4,5},{5,6},{6,7},{7,4},{8,9},{9,10},{10,1... | collective-permute-start | bytes 2752520 | tf_op jit(solution)/shard_map/ppermute | solution.py:28
  10.9 26.2 %collective-permute-start.3 = (bf16[128,3584]{1,0:T(8,128)(2,1)}, bf16[128,3584]{1,0:T(8,128)(2,1)}, u32[]{:S(2)}, u32[]{:S(2)}) collective-permute-start(bf16[128,3584]{1,0:T(8,128)(2,1)} %bitcast.5.own_ref), channel_id=1, source_target_pairs={{0,3},{1,0},{2,1},{3,2},{4,7},{5,4},{6,5},{7,6},{8,11},{9,8},{10,9... | collective-permute-start | bytes 2752520 | tf_op jit(solution)/shard_map/ppermute | solution.py:28
  16.0 0.9 copy-start.2
  16.9 11.9 %copy-start.4 = (bf16[4,2,2,128,128]{4,3,2,1,0:T(8,128)(2,1)}, bf16[4,2,2,128,128]{4,3,2,1,0:T(8,128)(2,1)S(1)}, u32[]{:S(2)}) copy-start(bf16[4,2,2,128,128]{4,3,2,1,0:T(8,128)(2,1)S(1)} %all-to-all-done.saved_ref) | copy-start | bytes 1572868
  16.9 38.3 %all-to-all-start.1 = ((bf16[8,16,3712]{2,1,0:T(8,128)(2,1)}), bf16[8,16,3712]{2,1,0:T(8,128)(2,1)S(1)}, u32[]{:S(2)}, u32[]{:S(2)}) async-start(bf16[8,16,3712]{2,1,0:T(8,128)(2,1)} %copy-done.2), calls=%async_computation.1 | async-start | bytes 1900544 | tf_op jit(solution)/shard_map/all_to_all | solution.py:320
  29.8 29.6 %collective-permute-start.6 = (bf16[2,1792,128]{2,1,0:T(8,128)(2,1)}, bf16[2,1792,128]{2,1,0:T(8,128)(2,1)}, u32[]{:S(2)}, u32[]{:S(2)}) collective-permute-start(bf16[2,1792,128]{2,1,0:T(8,128)(2,1)} %pad_maximum_fusion.1.own_ref), channel_id=1, source_target_pairs={{0,1},{1,2},{2,3},{3,0},{4,5},{5,6},{6,7},{7,4},{8,9},{9,10},{10,1... | collective-permute-start | bytes 2752520 | tf_op jit(solution)/shard_map/ppermute | solution.py:28
  32.6 31.6 %collective-permute-start.7 = (bf16[2,1792,128]{2,1,0:T(8,128)(2,1)}, bf16[2,1792,128]{2,1,0:T(8,128)(2,1)}, u32[]{:S(2)}, u32[]{:S(2)}) collective-permute-start(bf16[2,1792,128]{2,1,0:T(8,128)(2,1)} %pad_maximum_fusion.1.own_ref), channel_id=1, source_target_pairs={{0,3},{1,0},{2,1},{3,2},{4,7},{5,4},{6,5},{7,6},{8,11},{9,8},{10,9... | collective-permute-start | bytes 2752520 | tf_op jit(solution)/shard_map/ppermute | solution.py:28
  38.9 31.3 %collective-permute-start.4 = (bf16[64,3584]{1,0:T(8,128)(2,1)}, bf16[64,3584]{1,0:T(8,128)(2,1)}, u32[]{:S(2)}, u32[]{:S(2)}) collective-permute-start(bf16[64,3584]{1,0:T(8,128)(2,1)} %slice.56), channel_id=1, source_target_pairs={{0,1},{1,2},{2,3},{3,0},{4,5},{5,6},{6,7},{7,4},{8,9},{9,10},{10,1... | collective-permute-start | bytes 1376264 | tf_op jit(solution)/shard_map/ppermute | solution.py:28
  43.5 26.7 %collective-permute-start.5 = (bf16[64,3584]{1,0:T(8,128)(2,1)}, bf16[64,3584]{1,0:T(8,128)(2,1)}, u32[]{:S(2)}, u32[]{:S(2)}) collective-permute-start(bf16[64,3584]{1,0:T(8,128)(2,1)} %slice.57), channel_id=1, source_target_pairs={{0,3},{1,0},{2,1},{3,2},{4,7},{5,4},{6,5},{7,6},{8,11},{9,8},{10,9... | collective-permute-start | bytes 1376264 | tf_op jit(solution)/shard_map/ppermute | solution.py:28
  55.2 31.4 %all-to-all-start.2 = ((bf16[8,16,3712]{2,1,0:T(8,128)(2,1)}), bf16[8,16,3712]{2,1,0:T(8,128)(2,1)}, u32[]{:S(2)}, u32[]{:S(2)}) async-start(bf16[8,16,3712]{2,1,0:T(8,128)(2,1)} %get-tuple-element.20), calls=%async_computation.2 | async-start | bytes 1900544 | tf_op jit(solution)/shard_map/all_to_all | solution.py:320
  61.3 29.9 %collective-permute-start.12 = (bf16[1792,128]{1,0:T(8,128)(2,1)}, bf16[1792,128]{1,0:T(8,128)(2,1)}, u32[]{:S(2)}, u32[]{:S(2)}) collective-permute-start(bf16[1792,128]{1,0:T(8,128)(2,1)} %slice_bitcast_fusion.1), channel_id=1, source_target_pairs={{0,1},{1,2},{2,3},{3,0},{4,5},{5,6},{6,7},{7,4},{8,9},{9,10},{10,1... | collective-permute-start | bytes 1376264 | tf_op jit(solution)/shard_map/ppermute | solution.py:28
  66.0 25.2 %collective-permute-start.13 = (bf16[1792,128]{1,0:T(8,128)(2,1)}, bf16[1792,128]{1,0:T(8,128)(2,1)}, u32[]{:S(2)}, u32[]{:S(2)}) collective-permute-start(bf16[1792,128]{1,0:T(8,128)(2,1)} %slice_bitcast_fusion), channel_id=1, source_target_pairs={{0,3},{1,0},{2,1},{3,2},{4,7},{5,4},{6,5},{7,6},{8,11},{9,8},{10,9... | collective-permute-start | bytes 1376264 | tf_op jit(solution)/shard_map/ppermute | solution.py:28
  70.2 28.8 %collective-permute-start.8 = (bf16[2,1792,128]{2,1,0:T(8,128)(2,1)S(1)}, bf16[2,1792,128]{2,1,0:T(8,128)(2,1)}, u32[]{:S(2)}, u32[]{:S(2)}) collective-permute-start(bf16[2,1792,128]{2,1,0:T(8,128)(2,1)S(1)} %pad_maximum_fusion.own_ref), channel_id=1, source_target_pairs={{0,1},{1,2},{2,3},{3,0},{4,5},{5,6},{6,7},{7,4},{8,9},{9,10},{10,1... | collective-permute-start | bytes 2752520 | tf_op jit(solution)/shard_map/ppermute | solution.py:28
  72.2 30.7 %collective-permute-start.9 = (bf16[2,1792,128]{2,1,0:T(8,128)(2,1)S(1)}, bf16[2,1792,128]{2,1,0:T(8,128)(2,1)}, u32[]{:S(2)}, u32[]{:S(2)}) collective-permute-start(bf16[2,1792,128]{2,1,0:T(8,128)(2,1)S(1)} %pad_maximum_fusion.own_ref), channel_id=1, source_target_pairs={{0,3},{1,0},{2,1},{3,2},{4,7},{5,4},{6,5},{7,6},{8,11},{9,8},{10,9... | collective-permute-start | bytes 2752520 | tf_op jit(solution)/shard_map/ppermute | solution.py:28
  77.3 1.0 copy-start.5
  86.6 1.0 copy-start.6
  94.5 0.9 copy-start.3
  95.4 28.8 %all-to-all-start.4 = ((bf16[8,32,1792]{2,1,0:T(8,128)(2,1)}), bf16[8,32,1792]{2,1,0:T(8,128)(2,1)S(1)}, u32[]{:S(2)}, u32[]{:S(2)}) async-start(bf16[8,32,1792]{2,1,0:T(8,128)(2,1)} %copy-done.3), calls=%async_computation.4 | async-start | bytes 1835008 | tf_op jit(solution)/shard_map/all_to_all | solution.py:320
  100.0 14.4 %collective-permute-start.10 = (bf16[1792,128]{1,0:T(8,128)(2,1)S(1)}, bf16[1792,128]{1,0:T(8,128)(2,1)S(1)}, u32[]{:S(2)}, u32[]{:S(2)}) collective-permute-start(bf16[1792,128]{1,0:T(8,128)(2,1)S(1)} %slice_bitcast_fusion.3), channel_id=1, source_target_pairs={{0,1},{1,2},{2,3},{3,0},{4,5},{5,6},{6,7},{7,4},{8,9},{9,10},{10,1... | collective-permute-start | bytes 1376264 | tf_op jit(solution)/shard_map/ppermute | solution.py:28
  103.9 12.7 %collective-permute-start.11 = (bf16[1792,128]{1,0:T(8,128)(2,1)S(1)}, bf16[1792,128]{1,0:T(8,128)(2,1)S(1)}, u32[]{:S(2)}, u32[]{:S(2)}) collective-permute-start(bf16[1792,128]{1,0:T(8,128)(2,1)S(1)} %slice_bitcast_fusion.2), channel_id=1, source_target_pairs={{0,3},{1,0},{2,1},{3,2},{4,7},{5,4},{6,5},{7,6},{8,11},{9,8},{10,9... | collective-permute-start | bytes 1376264 | tf_op jit(solution)/shard_map/ppermute | solution.py:28
  117.1 0.9 copy-start.1
  124.2 29.9 %all-to-all-start.3 = ((bf16[8,32,1792]{2,1,0:T(8,128)(2,1)}), bf16[8,32,1792]{2,1,0:T(8,128)(2,1)S(1)}, u32[]{:S(2)}, u32[]{:S(2)}) async-start(bf16[8,32,1792]{2,1,0:T(8,128)(2,1)} %copy-done.1), calls=%async_computation.3 | async-start | bytes 1835008 | tf_op jit(solution)/shard_map/all_to_all | solution.py:320

commit v4 on v3

--- a/solution.py
+++ b/solution.py
@@ -13,7 +13,7 @@
 FLOPS = (10000000000, 1000000000)
 NEAR = 10**9
 RING = 4
-VMEM_LIMIT = 48 * 1024 * 1024
+VMEM_LIMIT = 24 * 1024 * 1024
 
 
 def shifted(value, axis, steps):

time: 157 us -> 157 us (level)
  no operation moved by 1% of the time
where the time goes in v4:
time: 157 us; the launch traced here: 155 us
  starting transfers between devices  68.7 us (44%)
  waiting for transfers between devices  49.6 us (32%)
  Pallas kernels  18.3 us (12%)
  local copies, waits for them, and re-layouts  17.3 us (11%)
    all_to_all x5, waiting for transfers between devices, exchange(): lax.all_to_all(value, 'expert', split_axis=0, concat_axis=0, axis_index_g...  43.6 us
    ppermute x12, starting transfers between devices, turned(): return lax.ppermute(value, 'expert', pairs)  42.3 us
    all_to_all x5, starting transfers between devices, exchange(): lax.all_to_all(value, 'expert', split_axis=0, concat_axis=0, axis_index_g...  25.9 us
    pallas_call x2, Pallas kernels, hidden_grads(): pl.pallas_call(functools.partial(hidden_kernel, way), in_specs=[pl.BlockS...  6.71 us
    ppermute x12, waiting for transfers between devices, turned(): return lax.ppermute(value, 'expert', pairs)  6.03 us
    unnamed x24, local copies, waits for them, and re-layouts  4.99 us
    squeeze x2, local copies, waits for them, and re-layouts, per_device(): af, ag = (turned(al[0], 1), turned(ar[1], RING - 1))  3.67 us
    slice x2, local copies, waits for them, and re-layouts, per_device(): wf, wg = (turned(wl[:half], 1), turned(wr[half:], RING - 1))  3.66 us
  transfers between devices with their start and end apart: 19, of which 6 were waited for; matrix products, arithmetic and copies ran while one was open for 8% of the time, Pallas kernels for 11%

profile of v4, /device:TPU:24, one launch (start us, length us, event | category | flops | bytes accessed | tf_op | source)
XLA Modules:
  0.0 155.4 jit_solution(11068692881020748111)
XLA Ops:
  0.0 1.3 slice_bitcast_fusion.4
  1.3 0.0 collective-permute-start
  1.3 0.5 collective-permute-start.1
  1.8 0.8 shard_map.92
  2.7 4.3 %all-to-all-start = ((bf16[4,2,2,128,128]{4,3,2,1,0:T(8,128)(2,1)}), bf16[4,2,2,128,128]{4,3,2,1,0:T(8,128)(2,1)S(1)}, u32[]{:S(2)}, u32[]{:S(2)}) async-start(bf16[4,2,2,128,128]{4,3,2,1,0:T(8,128)(2,1)} %shard_map.92), calls=%async_computation | async-start | bytes 1048576 | tf_op jit(solution)/shard_map/all_to_all | solution.py:320
  7.0 3.9 %collective-permute-start.2 = (bf16[128,3584]{1,0:T(8,128)(2,1)}, bf16[128,3584]{1,0:T(8,128)(2,1)}, u32[]{:S(2)}, u32[]{:S(2)}) collective-permute-start(bf16[128,3584]{1,0:T(8,128)(2,1)} %bitcast.5.own_ref), channel_id=1, source_target_pairs={{0,1},{1,2},{2,3},{3,0},{4,5},{5,6},{6,7},{7,4},{8,9},{9,10},{10,1... | collective-permute-start | bytes 2752520 | tf_op jit(solution)/shard_map/ppermute | solution.py:28
  10.9 3.1 %collective-permute-start.3 = (bf16[128,3584]{1,0:T(8,128)(2,1)}, bf16[128,3584]{1,0:T(8,128)(2,1)}, u32[]{:S(2)}, u32[]{:S(2)}) collective-permute-start(bf16[128,3584]{1,0:T(8,128)(2,1)} %bitcast.5.own_ref), channel_id=1, source_target_pairs={{0,3},{1,0},{2,1},{3,2},{4,7},{5,4},{6,5},{7,6},{8,11},{9,8},{10,9... | collective-permute-start | bytes 2752520 | tf_op jit(solution)/shard_map/ppermute | solution.py:28
  14.0 0.1 copy.14.routes_ref
  14.2 0.0 collective-permute-done.rest_0_.first_ref
  14.2 0.0 collective-permute-done.1.rest_1_.second_ref
  14.2 1.8 %shard_map.91 = (bf16[8,16,3712]{2,1,0:T(8,128)(2,1)S(1)}, bf16[8,16,3712]{2,1,0:T(8,128)(2,1)}) custom-call(s32[2,1,64,1]{3,2,1,0:T(8,128)S(1)} %copy.14.routes_ref, bf16[2,1,64]{2,1,0:T(2,128)(2,1)S(1)} %copy.12.probs_ref, bf16[64,3584]{1,0:T(8,128)(2,1)S(1)} %collective-permute-done.rest_0_.first_ref, ...), custom_call_target="tpu_custom_call" | custom-call | flops 100000000 | bytes 4000000 | tf_op jit(solution)/shard_map/pallas_call | solution.py:81
  16.0 0.9 copy-done.2
  16.9 0.0 all-to-all-done.saved_ref
  16.9 10.3 %all-to-all-start.1 = ((bf16[8,16,3712]{2,1,0:T(8,128)(2,1)}), bf16[8,16,3712]{2,1,0:T(8,128)(2,1)S(1)}, u32[]{:S(2)}, u32[]{:S(2)}) async-start(bf16[8,16,3712]{2,1,0:T(8,128)(2,1)} %copy-done.2), calls=%async_computation.1 | async-start | bytes 1900544 | tf_op jit(solution)/shard_map/all_to_all | solution.py:320
  27.3 1.6 fusion
  28.8 1.0 pad_maximum_fusion.1.own_ref
  29.8 2.7 %collective-permute-start.6 = (bf16[2,1792,128]{2,1,0:T(8,128)(2,1)}, bf16[2,1792,128]{2,1,0:T(8,128)(2,1)}, u32[]{:S(2)}, u32[]{:S(2)}) collective-permute-start(bf16[2,1792,128]{2,1,0:T(8,128)(2,1)} %pad_maximum_fusion.1.own_ref), channel_id=1, source_target_pairs={{0,1},{1,2},{2,3},{3,0},{4,5},{5,6},{6,7},{7,4},{8,9},{9,10},{10,1... | collective-permute-start | bytes 2752520 | tf_op jit(solution)/shard_map/ppermute | solution.py:28
  32.6 4.3 %collective-permute-start.7 = (bf16[2,1792,128]{2,1,0:T(8,128)(2,1)}, bf16[2,1792,128]{2,1,0:T(8,128)(2,1)}, u32[]{:S(2)}, u32[]{:S(2)}) collective-permute-start(bf16[2,1792,128]{2,1,0:T(8,128)(2,1)} %pad_maximum_fusion.1.own_ref), channel_id=1, source_target_pairs={{0,3},{1,0},{2,1},{3,2},{4,7},{5,4},{6,5},{7,6},{8,11},{9,8},{10,9... | collective-permute-start | bytes 2752520 | tf_op jit(solution)/shard_map/ppermute | solution.py:28
  36.9 0.1 pad_maximum_fusion.own_ref
  37.1 0.0 collective-permute-done.2.left_ref
  37.1 0.0 collective-permute-done.3.right_ref
  37.1 1.8 %slice.56 = bf16[64,3584]{1,0:T(8,128)(2,1)} slice(bf16[128,3584]{1,0:T(8,128)(2,1)} %collective-permute-done.2.left_ref), slice={[0:64], [0:3584]} | slice | bytes 917504 | tf_op jit(solution)/shard_map/slice | solution.py:333
  38.9 2.8 %collective-permute-start.4 = (bf16[64,3584]{1,0:T(8,128)(2,1)}, bf16[64,3584]{1,0:T(8,128)(2,1)}, u32[]{:S(2)}, u32[]{:S(2)}) collective-permute-start(bf16[64,3584]{1,0:T(8,128)(2,1)} %slice.56), channel_id=1, source_target_pairs={{0,1},{1,2},{2,3},{3,0},{4,5},{5,6},{6,7},{7,4},{8,9},{9,10},{10,1... | collective-permute-start | bytes 1376264 | tf_op jit(solution)/shard_map/ppermute | solution.py:28
  41.7 1.8 %slice.57 = bf16[64,3584]{1,0:T(8,128)(2,1)} slice(bf16[128,3584]{1,0:T(8,128)(2,1)} %collective-permute-done.3.right_ref), slice={[64:128], [0:3584]} | slice | bytes 917504 | tf_op jit(solution)/shard_map/slice | solution.py:333
  43.5 4.2 %collective-permute-start.5 = (bf16[64,3584]{1,0:T(8,128)(2,1)}, bf16[64,3584]{1,0:T(8,128)(2,1)}, u32[]{:S(2)}, u32[]{:S(2)}) collective-permute-start(bf16[64,3584]{1,0:T(8,128)(2,1)} %slice.57), channel_id=1, source_target_pairs={{0,3},{1,0},{2,1},{3,2},{4,7},{5,4},{6,5},{7,6},{8,11},{9,8},{10,9... | collective-permute-start | bytes 1376264 | tf_op jit(solution)/shard_map/ppermute | solution.py:28
  47.8 7.4 %all-to-all-done.1.tok_ref = bf16[8,16,3712]{2,1,0:T(8,128)(2,1)S(1)} async-done(((bf16[8,16,3712]{2,1,0:T(8,128)(2,1)}), bf16[8,16,3712]{2,1,0:T(8,128)(2,1)S(1)}, u32[]{:S(2)}, u32[]{:S(2)}) %all-to-all-start.1) | async-done | bytes 950304 | tf_op jit(solution)/shard_map/all_to_all | solution.py:320
  55.2 4.2 %all-to-all-start.2 = ((bf16[8,16,3712]{2,1,0:T(8,128)(2,1)}), bf16[8,16,3712]{2,1,0:T(8,128)(2,1)}, u32[]{:S(2)}, u32[]{:S(2)}) async-start(bf16[8,16,3712]{2,1,0:T(8,128)(2,1)} %get-tuple-element.20), calls=%async_computation.2 | async-start | bytes 1900544 | tf_op jit(solution)/shard_map/all_to_all | solution.py:320
  59.5 0.0 collective-permute-done.6.left_ref
  59.5 1.8 %slice_bitcast_fusion.1 = bf16[1792,128]{1,0:T(8,128)(2,1)} fusion(bf16[2,1792,128]{2,1,0:T(8,128)(2,1)} %collective-permute-done.6.left_ref), kind=kLoop, calls=%fused_computation.3 | loop fusion | bytes 917504 | tf_op jit(solution)/shard_map/squeeze | solution.py:338
  61.3 2.9 %collective-permute-start.12 = (bf16[1792,128]{1,0:T(8,128)(2,1)}, bf16[1792,128]{1,0:T(8,128)(2,1)}, u32[]{:S(2)}, u32[]{:S(2)}) collective-permute-start(bf16[1792,128]{1,0:T(8,128)(2,1)} %slice_bitcast_fusion.1), channel_id=1, source_target_pairs={{0,1},{1,2},{2,3},{3,0},{4,5},{5,6},{6,7},{7,4},{8,9},{9,10},{10,1... | collective-permute-start | bytes 1376264 | tf_op jit(solution)/shard_map/ppermute | solution.py:28
  64.2 0.0 collective-permute-done.7.right_ref
  64.2 1.8 %slice_bitcast_fusion = bf16[1792,128]{1,0:T(8,128)(2,1)} fusion(bf16[2,1792,128]{2,1,0:T(8,128)(2,1)} %collective-permute-done.7.right_ref), kind=kLoop, calls=%fused_computation.2 | loop fusion | bytes 917504 | tf_op jit(solution)/shard_map/squeeze | solution.py:338
  66.0 4.2 %collective-permute-start.13 = (bf16[1792,128]{1,0:T(8,128)(2,1)}, bf16[1792,128]{1,0:T(8,128)(2,1)}, u32[]{:S(2)}, u32[]{:S(2)}) collective-permute-start(bf16[1792,128]{1,0:T(8,128)(2,1)} %slice_bitcast_fusion), channel_id=1, source_target_pairs={{0,3},{1,0},{2,1},{3,2},{4,7},{5,4},{6,5},{7,6},{8,11},{9,8},{10,9... | collective-permute-start | bytes 1376264 | tf_op jit(solution)/shard_map/ppermute | solution.py:28
  70.2 0.0 collective-permute-done.4.low_ref
  70.2 0.0 collective-permute-done.5.high_ref
  70.2 1.9 %collective-permute-start.8 = (bf16[2,1792,128]{2,1,0:T(8,128)(2,1)S(1)}, bf16[2,1792,128]{2,1,0:T(8,128)(2,1)}, u32[]{:S(2)}, u32[]{:S(2)}) collective-permute-start(bf16[2,1792,128]{2,1,0:T(8,128)(2,1)S(1)} %pad_maximum_fusion.own_ref), channel_id=1, source_target_pairs={{0,1},{1,2},{2,3},{3,0},{4,5},{5,6},{6,7},{7,4},{8,9},{9,10},{10,1... | collective-permute-start | bytes 2752520 | tf_op jit(solution)/shard_map/ppermute | solution.py:28
  72.2 5.1 %collective-permute-start.9 = (bf16[2,1792,128]{2,1,0:T(8,128)(2,1)S(1)}, bf16[2,1792,128]{2,1,0:T(8,128)(2,1)}, u32[]{:S(2)}, u32[]{:S(2)}) collective-permute-start(bf16[2,1792,128]{2,1,0:T(8,128)(2,1)S(1)} %pad_maximum_fusion.own_ref), channel_id=1, source_target_pairs={{0,3},{1,0},{2,1},{3,2},{4,7},{5,4},{6,5},{7,6},{8,11},{9,8},{10,9... | collective-permute-start | bytes 2752520 | tf_op jit(solution)/shard_map/ppermute | solution.py:28
  77.3 1.0 copy-done.5
  78.3 3.2 %shard_map.93 = (bf16[128,1024]{1,0:T(8,128)(2,1)S(1)}, f32[128,128]{1,0:T(8,128)S(1)}) custom-call(s32[1]{0:T(128)} %bitcast.2.place_ref, bf16[8,16,3712]{2,1,0:T(8,128)(2,1)S(1)} %all-to-all-done.1.tok_ref, bf16[4,2,2,128,128]{4,3,2,1,0:T(8,128)(2,1)S(1)} %copy-done.5, bf16[128,3584]{1,0:T(8,128)(2,1)} %bitcast.5.own_ref, ...), custom_call_target="tpu_custom_call" | custom-call | flops 10000000000 | bytes 5000000 | tf_op jit(solution)/shard_map/pallas_call | solution.py:141
  81.6 5.1 %all-to-all-done.2.tok_ref = bf16[8,16,3712]{2,1,0:T(8,128)(2,1)} async-done(((bf16[8,16,3712]{2,1,0:T(8,128)(2,1)}), bf16[8,16,3712]{2,1,0:T(8,128)(2,1)}, u32[]{:S(2)}, u32[]{:S(2)}) %all-to-all-start.2) | async-done | bytes 950304 | tf_op jit(solution)/shard_map/all_to_all | solution.py:320
  86.7 1.0 copy-done.6
  87.7 3.5 %shard_map.94 = (bf16[128,1024]{1,0:T(8,128)(2,1)S(1)}, f32[128,128]{1,0:T(8,128)S(1)}) custom-call(s32[1]{0:T(128)} %bitcast.2.place_ref, bf16[8,16,3712]{2,1,0:T(8,128)(2,1)} %all-to-all-done.2.tok_ref, bf16[4,2,2,128,128]{4,3,2,1,0:T(8,128)(2,1)S(1)} %copy-done.6, bf16[128,3584]{1,0:T(8,128)(2,1)} %bitcast.5.own_ref, ...), custom_call_target="tpu_custom_call" | custom-call | flops 10000000000 | bytes 5000000 | tf_op jit(solution)/shard_map/pallas_call | solution.py:141
  91.2 0.0 collective-permute-done.12.gate_ref
  91.2 0.0 collective-permute-done.13.up_ref
  91.2 3.3 %shard_map.97 = bf16[8,32,1792]{2,1,0:T(8,128)(2,1)S(1)} custom-call(bf16[128,1024]{1,0:T(8,128)(2,1)S(1)} %get-tuple-element.18.first_ref, f32[128,128]{1,0:T(8,128)S(1)} %get-tuple-element.22.first_scaled_ref, bf16[128,1024]{1,0:T(8,128)(2,1)S(1)} %get-tuple-element.21.second_ref, f32[128,128]{1,0:T(8,128)S(1)} %get-tuple-element.23.second_scaled_ref, ...), custom_call_target="tpu_custom_call" | custom-call | flops 10000000000 | bytes 5000000 | tf_op jit(solution)/shard_map/pallas_call | solution.py:199
  94.5 0.0 copy-start.3
  94.5 0.9 copy-done.3
  95.4 3.6 %all-to-all-start.4 = ((bf16[8,32,1792]{2,1,0:T(8,128)(2,1)}), bf16[8,32,1792]{2,1,0:T(8,128)(2,1)S(1)}, u32[]{:S(2)}, u32[]{:S(2)}) async-start(bf16[8,32,1792]{2,1,0:T(8,128)(2,1)} %copy-done.3), calls=%async_computation.4 | async-start | bytes 1835008 | tf_op jit(solution)/shard_map/all_to_all | solution.py:320
  99.0 0.0 collective-permute-done.8.left_ref
  99.0 1.0 slice_bitcast_fusion.3
  100.0 2.8 %collective-permute-start.10 = (bf16[1792,128]{1,0:T(8,128)(2,1)S(1)}, bf16[1792,128]{1,0:T(8,128)(2,1)S(1)}, u32[]{:S(2)}, u32[]{:S(2)}) collective-permute-start(bf16[1792,128]{1,0:T(8,128)(2,1)S(1)} %slice_bitcast_fusion.3), channel_id=1, source_target_pairs={{0,1},{1,2},{2,3},{3,0},{4,5},{5,6},{6,7},{7,4},{8,9},{9,10},{10,1... | collective-permute-start | bytes 1376264 | tf_op jit(solution)/shard_map/ppermute | solution.py:28
  102.9 0.0 collective-permute-done.9.right_ref
  102.9 1.1 slice_bitcast_fusion.2
  103.9 4.2 %collective-permute-start.11 = (bf16[1792,128]{1,0:T(8,128)(2,1)S(1)}, bf16[1792,128]{1,0:T(8,128)(2,1)S(1)}, u32[]{:S(2)}, u32[]{:S(2)}) collective-permute-start(bf16[1792,128]{1,0:T(8,128)(2,1)S(1)} %slice_bitcast_fusion.2), channel_id=1, source_target_pairs={{0,3},{1,0},{2,1},{3,2},{4,7},{5,4},{6,5},{7,6},{8,11},{9,8},{10,9... | collective-permute-start | bytes 1376264 | tf_op jit(solution)/shard_map/ppermute | solution.py:28
  108.2 2.5 %shard_map.95.near_ref = f32[256,1792]{1,0:T(8,128)S(1)} custom-call(bf16[128,1024]{1,0:T(8,128)(2,1)S(1)} %get-tuple-element.18.first_ref, f32[128,128]{1,0:T(8,128)S(1)} %get-tuple-element.22.first_scaled_ref, bf16[128,1024]{1,0:T(8,128)(2,1)S(1)} %get-tuple-element.21.second_ref, f32[128,128]{1,0:T(8,128)S(1)} %get-tuple-element.23.second_scaled_ref, ...), custom_call_target="tpu_custom_call" | custom-call | flops 1000000000 | bytes 5000000 | tf_op jit(solution)/shard_map/pallas_call | solution.py:256
  110.7 3.8 %collective-permute-done.10.gate_ref = bf16[1792,128]{1,0:T(8,128)(2,1)S(1)} collective-permute-done((bf16[1792,128]{1,0:T(8,128)(2,1)S(1)}, bf16[1792,128]{1,0:T(8,128)(2,1)S(1)}, u32[]{:S(2)}, u32[]{:S(2)}) %collective-permute-start.10) | collective-permute-done | bytes 458784 | tf_op jit(solution)/shard_map/ppermute | solution.py:28
  114.4 2.2 %collective-permute-done.11.up_ref = bf16[1792,128]{1,0:T(8,128)(2,1)S(1)} collective-permute-done((bf16[1792,128]{1,0:T(8,128)(2,1)S(1)}, bf16[1792,128]{1,0:T(8,128)(2,1)S(1)}, u32[]{:S(2)}, u32[]{:S(2)}) %collective-permute-start.11) | collective-permute-done | bytes 458784 | tf_op jit(solution)/shard_map/ppermute | solution.py:28
  116.7 0.5 shard_map.96
  117.1 0.9 copy-done.1
  118.1 6.1 %all-to-all-done.4.back_ref = bf16[8,32,1792]{2,1,0:T(8,128)(2,1)S(1)} async-done(((bf16[8,32,1792]{2,1,0:T(8,128)(2,1)}), bf16[8,32,1792]{2,1,0:T(8,128)(2,1)S(1)}, u32[]{:S(2)}, u32[]{:S(2)}) %all-to-all-start.4) | async-done | bytes 917536 | tf_op jit(solution)/shard_map/all_to_all | solution.py:320
  124.2 3.6 %all-to-all-start.3 = ((bf16[8,32,1792]{2,1,0:T(8,128)(2,1)}), bf16[8,32,1792]{2,1,0:T(8,128)(2,1)S(1)}, u32[]{:S(2)}, u32[]{:S(2)}) async-start(bf16[8,32,1792]{2,1,0:T(8,128)(2,1)} %copy-done.1), calls=%async_computation.3 | async-start | bytes 1835008 | tf_op jit(solution)/shard_map/all_to_all | solution.py:320
  127.7 1.4 shard_map.98.rest_0_
  129.1 24.9 %all-to-all-done.3.back_ref = bf16[8,32,1792]{2,1,0:T(8,128)(2,1)S(1)} async-done(((bf16[8,32,1792]{2,1,0:T(8,128)(2,1)}), bf16[8,32,1792]{2,1,0:T(8,128)(2,1)S(1)}, u32[]{:S(2)}, u32[]{:S(2)}) %all-to-all-start.3) | async-done | bytes 917536 | tf_op jit(solution)/shard_map/all_to_all | solution.py:320
  154.0 1.4 shard_map.99
  (19 shorter events, 0.1 us)
Async XLA Ops:
  0.0 37.0 %copy-start = (f32[1,3584,4]{1,2,0:T(4,128)S(1)}, f32[1,3584,4]{1,2,0:T(4,128)}, u32[]{:S(2)}) copy-start(f32[1,3584,4]{1,2,0:T(4,128)} %param.17) | copy-start | bytes 172036
  0.0 1.8 %copy-start.7 = (bf16[2,1,1,32,16,128]{5,4,3,2,1,0:T(8,128)(2,1)S(1)}, bf16[2,1,1,32,16,128]{5,4,3,2,1,0:T(8,128)(2,1)}, u32[]{:S(2)}) copy-start(bf16[2,1,1,32,16,128]{5,4,3,2,1,0:T(8,128)(2,1)} %param.12) | copy-start | bytes 786436
  0.0 1.8 %copy-start.8 = (bf16[2,1,1,32,16,128]{5,4,3,2,1,0:T(8,128)(2,1)S(1)}, bf16[2,1,1,32,16,128]{5,4,3,2,1,0:T(8,128)(2,1)}, u32[]{:S(2)}) copy-start(bf16[2,1,1,32,16,128]{5,4,3,2,1,0:T(8,128)(2,1)} %param.13) | copy-start | bytes 786436
  0.0 14.0 %copy-start.9 = (s32[2,1,64,1]{2,3,1,0:T(1,128)S(1)}, s32[2,1,64,1]{2,3,1,0:T(1,128)}, u32[]{:S(2)}) copy-start(s32[2,1,64,1]{2,3,1,0:T(1,128)} %param.10) | copy-start | bytes 1540
  0.0 14.1 %copy-start.10 = (bf16[2,1,64]{2,0,1:T(2,128)(2,1)S(1)}, bf16[2,1,64]{2,0,1:T(2,128)(2,1)}, u32[]{:S(2)}) copy-start(bf16[2,1,64]{2,0,1:T(2,128)(2,1)} %param.11) | copy-start | bytes 772
  1.3 12.9 %collective-permute-start = (bf16[64,3584]{1,0:T(8,128)(2,1)S(1)}, bf16[64,3584]{1,0:T(8,128)(2,1)S(1)}, u32[]{:S(2)}, u32[]{:S(2)}) collective-permute-start(bf16[64,3584]{1,0:T(8,128)(2,1)S(1)} %get-tuple-element.30), channel_id=1, source_target_pairs={{0,480},{32,0},{64,32},{96,64},{128,96},{160,128},{192,160},{224,1... | collective-permute-start | bytes 1376264 | tf_op jit(solution)/shard_map/ppermute | solution.py:22
  1.3 12.9 %collective-permute-start.1 = (bf16[64,3584]{1,0:T(8,128)(2,1)S(1)}, bf16[64,3584]{1,0:T(8,128)(2,1)S(1)}, u32[]{:S(2)}, u32[]{:S(2)}) collective-permute-start(bf16[64,3584]{1,0:T(8,128)(2,1)S(1)} %get-tuple-element.29), channel_id=1, source_target_pairs={{0,32},{32,64},{64,96},{96,128},{128,160},{160,192},{192,224},{224... | collective-permute-start | bytes 1376264 | tf_op jit(solution)/shard_map/ppermute | solution.py:22
  2.7 14.3 %all-to-all-start = ((bf16[4,2,2,128,128]{4,3,2,1,0:T(8,128)(2,1)}), bf16[4,2,2,128,128]{4,3,2,1,0:T(8,128)(2,1)S(1)}, u32[]{:S(2)}, u32[]{:S(2)}) async-start(bf16[4,2,2,128,128]{4,3,2,1,0:T(8,128)(2,1)} %shard_map.92), calls=%async_computation | async-start | bytes 1048576 | tf_op jit(solution)/shard_map/all_to_all | solution.py:320
  7.0 30.1 %collective-permute-start.2 = (bf16[128,3584]{1,0:T(8,128)(2,1)}, bf16[128,3584]{1,0:T(8,128)(2,1)}, u32[]{:S(2)}, u32[]{:S(2)}) collective-permute-start(bf16[128,3584]{1,0:T(8,128)(2,1)} %bitcast.5.own_ref), channel_id=1, source_target_pairs={{0,1},{1,2},{2,3},{3,0},{4,5},{5,6},{6,7},{7,4},{8,9},{9,10},{10,1... | collective-permute-start | bytes 2752520 | tf_op jit(solution)/shard_map/ppermute | solution.py:28
  10.9 26.2 %collective-permute-start.3 = (bf16[128,3584]{1,0:T(8,128)(2,1)}, bf16[128,3584]{1,0:T(8,128)(2,1)}, u32[]{:S(2)}, u32[]{:S(2)}) collective-permute-start(bf16[128,3584]{1,0:T(8,128)(2,1)} %bitcast.5.own_ref), channel_id=1, source_target_pairs={{0,3},{1,0},{2,1},{3,2},{4,7},{5,4},{6,5},{7,6},{8,11},{9,8},{10,9... | collective-permute-start | bytes 2752520 | tf_op jit(solution)/shard_map/ppermute | solution.py:28
  16.0 0.9 copy-start.2
  16.9 11.9 %copy-start.4 = (bf16[4,2,2,128,128]{4,3,2,1,0:T(8,128)(2,1)}, bf16[4,2,2,128,128]{4,3,2,1,0:T(8,128)(2,1)S(1)}, u32[]{:S(2)}) copy-start(bf16[4,2,2,128,128]{4,3,2,1,0:T(8,128)(2,1)S(1)} %all-to-all-done.saved_ref) | copy-start | bytes 1572868
  16.9 38.3 %all-to-all-start.1 = ((bf16[8,16,3712]{2,1,0:T(8,128)(2,1)}), bf16[8,16,3712]{2,1,0:T(8,128)(2,1)S(1)}, u32[]{:S(2)}, u32[]{:S(2)}) async-start(bf16[8,16,3712]{2,1,0:T(8,128)(2,1)} %copy-done.2), calls=%async_computation.1 | async-start | bytes 1900544 | tf_op jit(solution)/shard_map/all_to_all | solution.py:320
  29.8 29.6 %collective-permute-start.6 = (bf16[2,1792,128]{2,1,0:T(8,128)(2,1)}, bf16[2,1792,128]{2,1,0:T(8,128)(2,1)}, u32[]{:S(2)}, u32[]{:S(2)}) collective-permute-start(bf16[2,1792,128]{2,1,0:T(8,128)(2,1)} %pad_maximum_fusion.1.own_ref), channel_id=1, source_target_pairs={{0,1},{1,2},{2,3},{3,0},{4,5},{5,6},{6,7},{7,4},{8,9},{9,10},{10,1... | collective-permute-start | bytes 2752520 | tf_op jit(solution)/shard_map/ppermute | solution.py:28
  32.6 31.6 %collective-permute-start.7 = (bf16[2,1792,128]{2,1,0:T(8,128)(2,1)}, bf16[2,1792,128]{2,1,0:T(8,128)(2,1)}, u32[]{:S(2)}, u32[]{:S(2)}) collective-permute-start(bf16[2,1792,128]{2,1,0:T(8,128)(2,1)} %pad_maximum_fusion.1.own_ref), channel_id=1, source_target_pairs={{0,3},{1,0},{2,1},{3,2},{4,7},{5,4},{6,5},{7,6},{8,11},{9,8},{10,9... | collective-permute-start | bytes 2752520 | tf_op jit(solution)/shard_map/ppermute | solution.py:28
  38.9 31.3 %collective-permute-start.4 = (bf16[64,3584]{1,0:T(8,128)(2,1)}, bf16[64,3584]{1,0:T(8,128)(2,1)}, u32[]{:S(2)}, u32[]{:S(2)}) collective-permute-start(bf16[64,3584]{1,0:T(8,128)(2,1)} %slice.56), channel_id=1, source_target_pairs={{0,1},{1,2},{2,3},{3,0},{4,5},{5,6},{6,7},{7,4},{8,9},{9,10},{10,1... | collective-permute-start | bytes 1376264 | tf_op jit(solution)/shard_map/ppermute | solution.py:28
  43.5 26.7 %collective-permute-start.5 = (bf16[64,3584]{1,0:T(8,128)(2,1)}, bf16[64,3584]{1,0:T(8,128)(2,1)}, u32[]{:S(2)}, u32[]{:S(2)}) collective-permute-start(bf16[64,3584]{1,0:T(8,128)(2,1)} %slice.57), channel_id=1, source_target_pairs={{0,3},{1,0},{2,1},{3,2},{4,7},{5,4},{6,5},{7,6},{8,11},{9,8},{10,9... | collective-permute-start | bytes 1376264 | tf_op jit(solution)/shard_map/ppermute | solution.py:28
  55.2 31.4 %all-to-all-start.2 = ((bf16[8,16,3712]{2,1,0:T(8,128)(2,1)}), bf16[8,16,3712]{2,1,0:T(8,128)(2,1)}, u32[]{:S(2)}, u32[]{:S(2)}) async-start(bf16[8,16,3712]{2,1,0:T(8,128)(2,1)} %get-tuple-element.20), calls=%async_computation.2 | async-start | bytes 1900544 | tf_op jit(solution)/shard_map/all_to_all | solution.py:320
  61.3 29.9 %collective-permute-start.12 = (bf16[1792,128]{1,0:T(8,128)(2,1)}, bf16[1792,128]{1,0:T(8,128)(2,1)}, u32[]{:S(2)}, u32[]{:S(2)}) collective-permute-start(bf16[1792,128]{1,0:T(8,128)(2,1)} %slice_bitcast_fusion.1), channel_id=1, source_target_pairs={{0,1},{1,2},{2,3},{3,0},{4,5},{5,6},{6,7},{7,4},{8,9},{9,10},{10,1... | collective-permute-start | bytes 1376264 | tf_op jit(solution)/shard_map/ppermute | solution.py:28
  66.0 25.2 %collective-permute-start.13 = (bf16[1792,128]{1,0:T(8,128)(2,1)}, bf16[1792,128]{1,0:T(8,128)(2,1)}, u32[]{:S(2)}, u32[]{:S(2)}) collective-permute-start(bf16[1792,128]{1,0:T(8,128)(2,1)} %slice_bitcast_fusion), channel_id=1, source_target_pairs={{0,3},{1,0},{2,1},{3,2},{4,7},{5,4},{6,5},{7,6},{8,11},{9,8},{10,9... | collective-permute-start | bytes 1376264 | tf_op jit(solution)/shard_map/ppermute | solution.py:28
  70.2 28.8 %collective-permute-start.8 = (bf16[2,1792,128]{2,1,0:T(8,128)(2,1)S(1)}, bf16[2,1792,128]{2,1,0:T(8,128)(2,1)}, u32[]{:S(2)}, u32[]{:S(2)}) collective-permute-start(bf16[2,1792,128]{2,1,0:T(8,128)(2,1)S(1)} %pad_maximum_fusion.own_ref), channel_id=1, source_target_pairs={{0,1},{1,2},{2,3},{3,0},{4,5},{5,6},{6,7},{7,4},{8,9},{9,10},{10,1... | collective-permute-start | bytes 2752520 | tf_op jit(solution)/shard_map/ppermute | solution.py:28
  72.2 30.7 %collective-permute-start.9 = (bf16[2,1792,128]{2,1,0:T(8,128)(2,1)S(1)}, bf16[2,1792,128]{2,1,0:T(8,128)(2,1)}, u32[]{:S(2)}, u32[]{:S(2)}) collective-permute-start(bf16[2,1792,128]{2,1,0:T(8,128)(2,1)S(1)} %pad_maximum_fusion.own_ref), channel_id=1, source_target_pairs={{0,3},{1,0},{2,1},{3,2},{4,7},{5,4},{6,5},{7,6},{8,11},{9,8},{10,9... | collective-permute-start | bytes 2752520 | tf_op jit(solution)/shard_map/ppermute | solution.py:28
  77.3 1.0 copy-start.5
  86.6 1.0 copy-start.6
  94.5 0.9 copy-start.3
  95.4 28.8 %all-to-all-start.4 = ((bf16[8,32,1792]{2,1,0:T(8,128)(2,1)}), bf16[8,32,1792]{2,1,0:T(8,128)(2,1)S(1)}, u32[]{:S(2)}, u32[]{:S(2)}) async-start(bf16[8,32,1792]{2,1,0:T(8,128)(2,1)} %copy-done.3), calls=%async_computation.4 | async-start | bytes 1835008 | tf_op jit(solution)/shard_map/all_to_all | solution.py:320
  100.0 14.4 %collective-permute-start.10 = (bf16[1792,128]{1,0:T(8,128)(2,1)S(1)}, bf16[1792,128]{1,0:T(8,128)(2,1)S(1)}, u32[]{:S(2)}, u32[]{:S(2)}) collective-permute-start(bf16[1792,128]{1,0:T(8,128)(2,1)S(1)} %slice_bitcast_fusion.3), channel_id=1, source_target_pairs={{0,1},{1,2},{2,3},{3,0},{4,5},{5,6},{6,7},{7,4},{8,9},{9,10},{10,1... | collective-permute-start | bytes 1376264 | tf_op jit(solution)/shard_map/ppermute | solution.py:28
  103.9 12.7 %collective-permute-start.11 = (bf16[1792,128]{1,0:T(8,128)(2,1)S(1)}, bf16[1792,128]{1,0:T(8,128)(2,1)S(1)}, u32[]{:S(2)}, u32[]{:S(2)}) collective-permute-start(bf16[1792,128]{1,0:T(8,128)(2,1)S(1)} %slice_bitcast_fusion.2), channel_id=1, source_target_pairs={{0,3},{1,0},{2,1},{3,2},{4,7},{5,4},{6,5},{7,6},{8,11},{9,8},{10,9... | collective-permute-start | bytes 1376264 | tf_op jit(solution)/shard_map/ppermute | solution.py:28
  117.1 0.9 copy-start.1
  124.2 29.9 %all-to-all-start.3 = ((bf16[8,32,1792]{2,1,0:T(8,128)(2,1)}), bf16[8,32,1792]{2,1,0:T(8,128)(2,1)S(1)}, u32[]{:S(2)}, u32[]{:S(2)}) async-start(bf16[8,32,1792]{2,1,0:T(8,128)(2,1)} %copy-done.1), calls=%async_computation.3 | async-start | bytes 1835008 | tf_op jit(solution)/shard_map/all_to_all | solution.py:320
